TPU v7x, 32 devices: a whole 2x2x4 slice. The times are simulated.
32 devices in a mesh: groups: 2 (over y), ctx: 4 (over z), dp: 2 (over x), mp: 2 (over core).
Axes of the slice: x: 2, y: 2, z: 4, core: 2. Of those that a mesh axis runs over, the one named last changes fastest.
Arguments:
- positions: int32 [4, 512], P(('groups', 'dp')), parts along dimension 0, may hold values from 0 to 4095, as said below
- queries: bfloat16 [4, 1024, 4096], P(('groups', 'dp'), 'ctx', 'mp'), parts along dimension 0, may hold values from -4 to 4
- keys: bfloat16 [4, 1024, 512], P(('groups', 'dp'), 'ctx', 'mp'), parts along dimension 0, may hold values from -36 to 36
- values: bfloat16 [4, 1024, 512], P(('groups', 'dp'), 'ctx', 'mp'), parts along dimension 0, may hold values from -6 to 6
- out_grad: bfloat16 [4, 1024, 4096], P(('groups', 'dp'), 'ctx', 'mp'), parts along dimension 0, may hold values from -6 to 6
Outputs:
- query_grad: bfloat16 [4, 1024, 4096], P(('groups', 'dp'), 'ctx', 'mp'), parts along dimension 0
- key_grad: bfloat16 [4, 1024, 512], P(('groups', 'dp'), 'ctx', 'mp'), parts along dimension 0
- value_grad: bfloat16 [4, 1024, 512], P(('groups', 'dp'), 'ctx', 'mp'), parts along dimension 0
There are 2 independent parts, one for each index of `groups`. A program takes and returns all parts, laid end to end along the dimension named above; each array names one. Nothing has to cross between parts.
Inputs may be any that keep to these rules, and one draw needn't show every extreme that they name: In each sequence the positions rise strictly with the rank; the shard k * 1024 to (k + 1) * 1024 - 1 holds at most 256 of them, and some shard holds exactly 256.
All inputs are finite; a program needn't handle non-finite values.
Results may differ from a plain program's by a relative error of at most 0.007.
The roundings to bfloat16 on the way count: a program that leaves them out, or rounds other values in their place, can miss the bound.
Values may be sent and summed in bfloat16 or wider, within the bound.
No kernel may reach another device: no remote copies, remote signals or barrier semaphores. Data moves between devices by JAX's collectives and lax.ppermute only.
A program may use at most 128 MiB of HBM per device.

v0:
```python
import functools
import math

import jax
import jax.numpy as jnp
import numpy as np
from jax import lax
from jax.experimental import pallas as pl
from jax.experimental.pallas import tpu as pltpu
from jax.sharding import PartitionSpec as P

HEAD_DIM = 128
HALF_DIM = HEAD_DIM // 2
TOK_SHARD = 1024
ROPE_BASE = 500000.0
SCORE_SCALE = 1.0 / math.sqrt(HEAD_DIM)
EXP2_SCALE = SCORE_SCALE * math.log2(math.e)
HIDDEN = -1e30
ALIGN = 16
CHUNK = 288
MIB = 1024 * 1024

VMEM = pl.BlockSpec(memory_space=pltpu.VMEM)
SMEM = pl.BlockSpec(memory_space=pltpu.SMEM)
HBM = pl.BlockSpec(memory_space=pltpu.HBM)


def vmem(routed, small, large):
    return pltpu.CompilerParams(vmem_limit_bytes=(small if routed <= 512 else large) * MIB)


def dot(left, right, contract):
    return lax.dot_general(left, right, (contract, ((), ())), preferred_element_type=jnp.float32)


def turn(field, cos_full, sin_full):
    return field * cos_full + pltpu.roll(field, HALF_DIM, 1) * sin_full


def turn_back(field, cos_full, sin_full):
    return field * cos_full - pltpu.roll(field, HALF_DIM, 1) * sin_full


def rope_rows():
    ladder = np.arange(HALF_DIM, dtype=np.float32)
    exponent = ladder * np.float32(-2.0 * math.log(ROPE_BASE) / HEAD_DIM)
    freq = np.exp(exponent.astype(np.float64)).astype(np.float32)
    sign = np.repeat(np.array([-1.0, 1.0], np.float32), HALF_DIM)
    return np.stack([np.concatenate([freq, freq]), sign])


def shard_layout(ctx_size, me, pos, meta_ref):
    shard_of = pos // TOK_SHARD
    for hop in range(2 * ctx_size):
        meta_ref[hop] = 0
    start = jnp.int32(0)
    first = jnp.int32(0)
    my_first = jnp.int32(0)
    for shard in range(ctx_size):
        count = jnp.sum(jnp.where(shard_of == shard, 1.0, 0.0)).astype(jnp.int32)
        my_first = jnp.where(me == shard, first, my_first)

        @pl.when(me >= shard)
        def _():
            meta_ref[me - shard] = start
            meta_ref[ctx_size + me - shard] = count

        first = first + count
        start = start + (count + ALIGN - 1) // ALIGN * ALIGN
    return my_first


def prepare_kernel(
    ctx_size, rows_hbm, pos_hbm, keys_hbm, values_hbm, meta_ref, cos_ref, sin_ref, sent_ref, turned_ref, *refs
):
    rows_ref, pos_ref, keys_ref, values_ref, sems = refs
    sources = (pos_hbm, rows_hbm, keys_hbm, values_hbm)
    targets = (pos_ref, rows_ref, keys_ref, values_ref)
    copies = [
        pltpu.make_async_copy(source, target, sems.at[index])
        for index, (source, target) in enumerate(zip(sources, targets))
    ]
    for copy in copies:
        copy.start()
    copies[0].wait()
    slots = keys_ref.shape[0]
    pos = pos_ref[...]
    my_first = shard_layout(ctx_size, lax.axis_index("ctx"), pos, meta_ref)
    shape = (slots, pos.shape[1])
    gap = lax.broadcasted_iota(jnp.int32, shape, 1) - lax.broadcasted_iota(jnp.int32, shape, 0)
    named = jnp.where(gap == my_first, pos.astype(jnp.float32), 0.0)
    copies[1].wait()
    angles = jnp.sum(named, axis=1, keepdims=True) * rows_ref[0:1, :]
    cos_full = jnp.cos(angles)
    sin_full = jnp.sin(angles) * rows_ref[1:2, :]
    cos_ref[...] = cos_full
    sin_ref[...] = sin_full
    copies[2].wait()
    copies[3].wait()
    for lane in range(0, keys_ref.shape[1], HEAD_DIM):
        lanes = slice(lane, lane + HEAD_DIM)
        key = turn(keys_ref[:, lanes].astype(jnp.float32), cos_full, sin_full)
        middle = 2 * lane + HEAD_DIM
        turned_ref[:, lanes] = key.astype(jnp.bfloat16)
        sent_ref[:, 2 * lane : middle] = key.astype(jnp.bfloat16)
        sent_ref[:, middle : middle + HEAD_DIM] = values_ref[:, lanes]


def prepare(positions, keys, values, ctx_size):
    slots, width = keys.shape
    rows = jnp.asarray(rope_rows())
    table = jax.ShapeDtypeStruct((slots, HEAD_DIM), jnp.float32)
    sent = jax.ShapeDtypeStruct((slots, 2 * width), jnp.bfloat16)
    operands = (rows, positions, keys, values)
    return pl.pallas_call(
        functools.partial(prepare_kernel, ctx_size),
        out_shape=(
            jax.ShapeDtypeStruct((2 * ctx_size,), jnp.int32),
            table,
            table,
            sent,
            jax.ShapeDtypeStruct((slots, width), jnp.bfloat16),
        ),
        in_specs=[HBM] * 4,
        out_specs=(SMEM, VMEM, VMEM, VMEM, VMEM),
        scratch_shapes=[pltpu.VMEM(operand.shape, operand.dtype) for operand in operands]
        + [pltpu.SemaphoreType.DMA((4,))],
        compiler_params=vmem(positions.shape[1], 60, 60),
        name="prepare",
    )(*operands)


def queries_kernel(
    cos_ref,
    sin_ref,
    query_ref,
    grad_ref,
    sent_ref,
    turned_ref,
    turned_t_ref,
    grad_t_ref,
    sent_again_ref,
):
    sent_again_ref[...] = sent_ref[...]
    for lane in range(0, query_ref.shape[1], HEAD_DIM):
        lanes = slice(lane, lane + HEAD_DIM)
        query = turn(query_ref[:, lanes].astype(jnp.float32), cos_ref[...], sin_ref[...])
        turned_ref[:, lanes] = query.astype(jnp.bfloat16)
        turned_t_ref[lanes, :] = query.T.astype(jnp.bfloat16)
        grad_t_ref[lanes, :] = grad_ref[:, lanes].astype(jnp.float32).T.astype(jnp.bfloat16)


def rotate_queries(cos_full, sin_full, queries, out_grad, sent):
    slots, width = queries.shape
    straight = jax.ShapeDtypeStruct((slots, width), jnp.bfloat16)
    across = jax.ShapeDtypeStruct((width, slots), jnp.bfloat16)
    return pl.pallas_call(
        queries_kernel,
        out_shape=(straight, across, across, jax.ShapeDtypeStruct(sent.shape, sent.dtype)),
        in_specs=[VMEM] * 5,
        out_specs=(VMEM,) * 4,
        compiler_params=vmem(0, 16, 16),
        cost_estimate=pl.CostEstimate(
            flops=3 * 10**9, bytes_accessed=4 * 1024 * 1024, transcendentals=0
        ),
        name="rotate_queries",
    )(cos_full, sin_full, queries, out_grad, sent)


def stacked(ref, lane, heads, width):
    parts = [ref[:width, lane + h * HEAD_DIM : lane + (h + 1) * HEAD_DIM] for h in range(heads)]
    return jnp.concatenate(parts, axis=0)


def beside(ref, rows, slots, width):
    if width == slots:
        return ref[:rows, :]
    parts = [ref[:rows, lane : lane + width] for lane in range(0, ref.shape[1], slots)]
    return jnp.concatenate(parts, axis=1)


def woven(keys, values):
    parts = []
    for lane in range(0, keys.shape[1], HEAD_DIM):
        parts += [keys[:, lane : lane + HEAD_DIM], values[:, lane : lane + HEAD_DIM]]
    return jnp.concatenate(parts, axis=1)


def terms_of(probs, score_grads, queries, grads):
    key_term = dot(score_grads, queries, ((1,), (0,))) * SCORE_SCALE
    return jnp.concatenate([key_term, dot(probs, grads, ((1,), (0,)))], axis=1)


def fold(field, join, reduce):
    while field.shape[0] % 16 == 0:
        half = field.shape[0] // 2
        field = join(field[:half], field[half:])
    return reduce(field, axis=0, keepdims=True)


def head_lanes(head):
    return slice(head * HEAD_DIM, (head + 1) * HEAD_DIM)


def key_lanes(key_head):
    return slice(2 * key_head * HEAD_DIM, (2 * key_head + 1) * HEAD_DIM)


def value_lanes(key_head):
    return slice((2 * key_head + 1) * HEAD_DIM, 2 * (key_head + 1) * HEAD_DIM)


def own_kernel(step_heads, sent_ref, turned_t_ref, grad_t_ref, weight_ref, product_ref, sums_ref, bias_ref):
    slots = sent_ref.shape[0]
    key_heads = sent_ref.shape[1] // HEAD_DIM // 2
    heads = turned_t_ref.shape[0] // HEAD_DIM // key_heads
    key_id = lax.broadcasted_iota(jnp.int32, (slots, slots), 0)
    slot_id = lax.broadcasted_iota(jnp.int32, (slots, slots), 1)
    bias_ref[...] = jnp.where(key_id <= slot_id, 0.0, HIDDEN)
    for key_head in range(key_heads):

        def step(index, carry):
            for part in range(step_heads):
                head = key_head * heads + index * step_heads + part
                rows = pl.ds(pl.multiple_of(head * HEAD_DIM, HEAD_DIM), HEAD_DIM)
                scores = dot(sent_ref[:, key_lanes(key_head)], turned_t_ref[rows, :], ((1,), (0,)))
                scores = scores + bias_ref[...]
                prob_grad = dot(sent_ref[:, value_lanes(key_head)], grad_t_ref[rows, :], ((1,), (0,)))
                peak = fold(scores, jnp.maximum, jnp.max)
                weights = jnp.exp2((scores - peak) * EXP2_SCALE)
                weight_ref[head] = weights
                product_ref[head] = prob_grad
                sums_ref[head, 0:1, :] = peak
                sums_ref[head, 1:2, :] = fold(weights, jnp.add, jnp.sum)
                sums_ref[head, 2:3, :] = fold(weights * prob_grad, jnp.add, jnp.sum)
            return carry

        lax.fori_loop(0, heads // step_heads, step, 0)


def own_scores(sent, turned_t, grad_t):
    slots = sent.shape[0]
    heads = turned_t.shape[0] // HEAD_DIM
    square = jax.ShapeDtypeStruct((heads, slots, slots), jnp.float32)
    return pl.pallas_call(
        functools.partial(own_kernel, 4),
        out_shape=(square, square, jax.ShapeDtypeStruct((heads, 8, slots), jnp.float32)),
        in_specs=[VMEM] * 3,
        out_specs=(VMEM,) * 3,
        scratch_shapes=[pltpu.VMEM((slots, slots), jnp.float32)],
        compiler_params=vmem(0, 16, 16),
        cost_estimate=pl.CostEstimate(
            flops=5 * 10**9, bytes_accessed=10 * 1024 * 1024, transcendentals=0
        ),
        name="own_scores",
    )(sent, turned_t, grad_t)


def scores_kernel(
    ctx_size,
    sizes,
    step_heads,
    meta_ref,
    turned_ref,
    grad_ref,
    turned_t_ref,
    grad_t_ref,
    sums_ref,
    *refs,
):
    inputs = refs[: -6 - ctx_size]
    refs = refs[len(inputs) :]
    terms, refs = refs[: ctx_size - 1], refs[ctx_size - 1 :]
    score_grad_ref, joined_ref, key_ref, value_ref, bias_ref, prob_ref, acc_ref = refs
    blocks = [block[...] for block in inputs]
    slots = turned_ref.shape[0]
    span = bias_ref.shape[0]
    key_heads = key_ref.shape[1] // HEAD_DIM
    heads = turned_ref.shape[1] // HEAD_DIM // key_heads
    starts = [pl.multiple_of(meta_ref[hop], ALIGN) for hop in range(ctx_size)]
    my_start, my_count = starts[0], meta_ref[ctx_size]
    sent_hops = list(range(1, ctx_size))
    if relayed(ctx_size):
        last = lax.axis_index("ctx") == ctx_size - 1
        alpha, beta, gamma, delta = woven(*blocks[:2]), blocks[2], blocks[3], woven(*blocks[4:])
        blocks = [jnp.where(last, alpha, gamma), jnp.where(last, beta, alpha), delta]
        sent_hops = [jnp.where(last, 3, 1), 2, jnp.where(last, 1, 2)]

    key_ref[slots:span, :] = jnp.zeros_like(key_ref[slots:span, :])
    value_ref[slots:span, :] = jnp.zeros_like(key_ref[slots:span, :])
    for hop in range(ctx_size - 1, 0, -1):
        for key_head in range(key_heads):
            lanes = head_lanes(key_head)
            key_ref[pl.ds(starts[hop], slots), lanes] = blocks[hop - 1][:, key_lanes(key_head)]
            value_ref[pl.ds(starts[hop], slots), lanes] = blocks[hop - 1][:, value_lanes(key_head)]
    place = lax.broadcasted_iota(jnp.int32, bias_ref.shape, 0)
    seen = place < 0
    for hop in range(1, ctx_size):
        end = starts[hop] + meta_ref[ctx_size + hop]
        seen = seen | ((place >= starts[hop]) & (place < end))
    bias_ref[...] = jnp.where(seen, 0.0, HIDDEN)
    live = lax.broadcasted_iota(jnp.int32, (1, slots), 1) < my_count

    def one_head(key_head, head, rows, width):
        place = key_head * heads + head
        lanes = pl.ds(pl.multiple_of(place * HEAD_DIM, HEAD_DIM), HEAD_DIM)
        columns = pl.ds(pl.multiple_of(head * slots, slots), width)
        bias = jnp.concatenate([bias_ref[:rows, :]] * (width // HEAD_DIM), axis=1)
        scores = dot(
            key_ref[:rows, head_lanes(key_head)], turned_t_ref[lanes, :width], ((1,), (0,))
        )
        scores = scores + bias
        prob_grad = dot(
            value_ref[:rows, head_lanes(key_head)], grad_t_ref[lanes, :width], ((1,), (0,))
        )
        own_peak = sums_ref[place, 0:1, :width]
        peak = jnp.maximum(own_peak, fold(scores, jnp.maximum, jnp.max))
        share = jnp.exp2((own_peak - peak) * EXP2_SCALE)
        weights = jnp.exp2((scores - peak) * EXP2_SCALE)
        total = sums_ref[place, 1:2, :width] * share + fold(weights, jnp.add, jnp.sum)
        inverse = 1.0 / total
        product = sums_ref[place, 2:3, :width] * share
        delta = (product + fold(weights * prob_grad, jnp.add, jnp.sum)) * inverse
        inverse = jnp.where(live[:, :width], inverse, 0.0)
        joined_ref[place, 0:1, :width] = share * inverse
        joined_ref[place, 1:2, :width] = delta
        prob = weights * inverse
        prob_ref[:rows, columns] = prob.astype(jnp.bfloat16)
        score_grad = (prob * (prob_grad - delta)).astype(jnp.bfloat16)
        score_grad_ref[key_head, :rows, columns] = score_grad
        if width < slots:
            rest = pl.ds(pl.multiple_of(head * slots + width, HEAD_DIM), slots - width)
            none = jnp.zeros((rows, slots - width), jnp.bfloat16)
            score_grad_ref[key_head, :rows, rest] = none
            joined_ref[place, 0:2, width:] = jnp.zeros((2, slots - width), jnp.float32)

    for key_head in range(key_heads):
        above = 0
        for rows, width in sizes:
            fits = (my_start > above) & (my_start <= rows)
            if width < slots:
                fits = (my_start > 0) & (my_count <= width)
            elif any(size[1] < slots for size in sizes):
                fits = fits & (my_count > sizes[-1][1])

            @pl.when(fits)
            def _():
                def step(index, carry):
                    for part in range(step_heads):
                        one_head(key_head, index * step_heads + part, rows, width)
                    return carry

                lax.fori_loop(0, heads // step_heads, step, 0)
                if rows % CHUNK:
                    beyond = slice(rows, rows + CHUNK - rows % CHUNK)
                    none = jnp.zeros((CHUNK - rows % CHUNK, heads * slots), jnp.bfloat16)
                    score_grad_ref[key_head, beyond, :] = none
                lane = key_head * heads * HEAD_DIM
                acc_ref[:rows, :] = terms_of(
                    beside(prob_ref, rows, slots, width),
                    beside(score_grad_ref.at[key_head], rows, slots, width),
                    stacked(turned_ref, lane, heads, width),
                    stacked(grad_ref, lane, heads, width),
                )

            above = rows if width == slots else above

        @pl.when(my_start == 0)
        def _():
            for place in range(key_head * heads, (key_head + 1) * heads):
                inverse = 1.0 / sums_ref[place, 1:2, :]
                joined_ref[place, 0:1, :] = jnp.where(live, inverse, 0.0)
                joined_ref[place, 1:2, :] = sums_ref[place, 2:3, :] * inverse

        for hop, term_ref in zip(sent_hops, terms):
            start = pl.multiple_of(meta_ref[hop], ALIGN)
            term = acc_ref[pl.ds(start, slots), :].astype(term_ref.dtype)
            term_ref[:, 2 * key_head * HEAD_DIM : 2 * (key_head + 1) * HEAD_DIM] = term


def relayed(ctx_size):
    return ctx_size == 4


def scores(meta, turned, out_grad, turned_t, grad_t, sums, blocks, routed, ctx_size):
    slots, width = blocks[0].shape
    if relayed(ctx_size):
        width = blocks[2].shape[1]
    key_heads = width // HEAD_DIM // 2
    heads = turned.shape[1] // HEAD_DIM // key_heads
    span = -(-(routed + ctx_size * ALIGN) // CHUNK) * CHUNK
    sizes, step_heads = [(span, slots)], 1
    if span == 2 * CHUNK and routed - slots // 2 + ctx_size * ALIGN <= 3 * CHUNK // 2 + ALIGN:
        sizes, step_heads = [(CHUNK, slots), (3 * CHUNK // 2, slots), (span, slots // 2)], 4
    terms = [jax.ShapeDtypeStruct((slots, width), jnp.bfloat16)] * (ctx_size - 1)
    if relayed(ctx_size):
        terms[2] = jax.ShapeDtypeStruct((slots, width), jnp.float32)
    outs = pl.pallas_call(
        functools.partial(scores_kernel, ctx_size, sizes, step_heads),
        out_shape=(
            *terms,
            jax.ShapeDtypeStruct((key_heads, span, heads * slots), jnp.bfloat16),
            jax.ShapeDtypeStruct((key_heads * heads, 8, slots), jnp.float32),
            jax.ShapeDtypeStruct((span + slots, key_heads * HEAD_DIM), jnp.bfloat16),
        ),
        in_specs=[SMEM] + [VMEM] * (5 + len(blocks)),
        out_specs=(VMEM,) * (ctx_size + 2),
        scratch_shapes=[
            pltpu.VMEM((span + slots, width // 2), jnp.bfloat16),
            pltpu.VMEM((span, HEAD_DIM), jnp.float32),
            pltpu.VMEM((span, heads * slots), jnp.bfloat16),
            pltpu.VMEM((span + slots, 2 * HEAD_DIM), jnp.float32),
        ],
        compiler_params=vmem(routed, 28, 60),
        cost_estimate=pl.CostEstimate(
            flops=8 * 10**9, bytes_accessed=12 * 1024 * 1024, transcendentals=0
        ),
        name="scores",
    )(meta, turned, out_grad, turned_t, grad_t, sums, *blocks)
    return outs[: ctx_size - 1], outs[ctx_size - 1 :]


def local_kernel(
    part,
    key_head,
    meta_ref,
    cos_ref,
    sin_ref,
    turned_ref,
    grad_ref,
    sent_ref,
    weight_ref,
    product_ref,
    score_grad_ref,
    joined_ref,
    key_ref,
    *refs,
):
    later = (len(refs) - 5) // 2
    dq_ref, own_ref = refs[later : later + 2]
    prob_ref, own_grad_ref, sum_ref = refs[-3:]
    for index in range(later):
        refs[later + 2 + index][...] = refs[index][...]
    slots = turned_ref.shape[0]
    heads = prob_ref.shape[1] // slots
    span = score_grad_ref.shape[1]
    my_start = meta_ref[0]
    own_key_t = sent_ref[:, key_lanes(key_head)].astype(jnp.float32).T.astype(jnp.bfloat16)
    for head in range(heads):
        columns = slice(head * slots, (head + 1) * slots)
        place = part * heads + head
        prob = weight_ref[key_head * heads + head] * joined_ref[place, 0:1, :]
        prob_ref[:, columns] = prob.astype(jnp.bfloat16)
        product = product_ref[key_head * heads + head] - joined_ref[place, 1:2, :]
        score_grad = (prob * product).astype(jnp.bfloat16)
        own_grad_ref[:, columns] = score_grad
        sum_ref[head] = dot(own_key_t, score_grad, ((1,), (0,)))
    for chunk in range(0, span, CHUNK):

        @pl.when(chunk < my_start)
        def _():
            rows = slice(chunk, chunk + CHUNK)
            key_t = key_ref[rows, head_lanes(part)].astype(jnp.float32).T.astype(jnp.bfloat16)
            for head in range(heads):
                columns = slice(head * slots, (head + 1) * slots)
                sum_ref[head] += dot(key_t, score_grad_ref[part, rows, columns], ((1,), (0,)))

    lane = key_head * heads * HEAD_DIM
    for head in range(heads):
        grad = turn_back((sum_ref[head] * SCORE_SCALE).T, cos_ref[...], sin_ref[...])
        dq_ref[:, head * HEAD_DIM : (head + 1) * HEAD_DIM] = grad.astype(jnp.bfloat16)
    own_ref[...] = terms_of(
        prob_ref[...],
        own_grad_ref[...],
        stacked(turned_ref, lane, heads, slots),
        stacked(grad_ref, lane, heads, slots),
    )


def local_terms(
    part, key_head, meta, cos_full, sin_full, turned, out_grad, sent, own, joined, later
):
    slots = turned.shape[0]
    heads = turned.shape[1] // (sent.shape[1] // 2)
    weight, product, _ = own
    operands = (meta, cos_full, sin_full, turned, out_grad, sent, weight, product, *joined, *later)
    return pl.pallas_call(
        functools.partial(local_kernel, part, key_head),
        out_shape=(
            jax.ShapeDtypeStruct((slots, heads * HEAD_DIM), jnp.bfloat16),
            jax.ShapeDtypeStruct((slots, 2 * HEAD_DIM), jnp.float32),
            *[jax.ShapeDtypeStruct(term.shape, term.dtype) for term in later],
        ),
        in_specs=[SMEM] + [VMEM] * (len(operands) - 1),
        out_specs=(VMEM,) * (2 + len(later)),
        scratch_shapes=[
            pltpu.VMEM((slots, heads * slots), jnp.bfloat16),
            pltpu.VMEM((slots, heads * slots), jnp.bfloat16),
            pltpu.VMEM((heads, HEAD_DIM, slots), jnp.float32),
        ],
        compiler_params=vmem(joined[0].shape[1] // 2, 16, 48),
        cost_estimate=pl.CostEstimate(
            flops=4 * 10**9, bytes_accessed=10 * 1024 * 1024, transcendentals=0
        ),
        name="local_terms",
    )(*operands)


def finish_kernel(ctx_size, meta_ref, cos_ref, sin_ref, *refs):
    key_grad_ref, value_grad_ref = refs[-2:]
    terms, owns = refs[: ctx_size - 1], refs[ctx_size - 1 : -2]
    slots = cos_ref.shape[0]
    live = lax.broadcasted_iota(jnp.int32, (slots, HEAD_DIM), 0) < meta_ref[ctx_size]
    total = jnp.concatenate([own[...] for own in owns], axis=1)
    for index, term in enumerate(terms):
        term = term[...].astype(jnp.float32)
        if index == 0 and relayed(ctx_size):
            term = jnp.where(lax.axis_index("ctx") == 2, 0.0, term)
        total += term
    for lane in range(0, key_grad_ref.shape[1], HEAD_DIM):
        lanes = slice(lane, lane + HEAD_DIM)
        key_term = turn_back(total[:, 2 * lane : 2 * lane + HEAD_DIM], cos_ref[...], sin_ref[...])
        value_term = total[:, 2 * lane + HEAD_DIM : 2 * (lane + HEAD_DIM)]
        key_grad_ref[:, lanes] = jnp.where(live, key_term, 0.0).astype(jnp.bfloat16)
        value_grad_ref[:, lanes] = jnp.where(live, value_term, 0.0).astype(jnp.bfloat16)


def finish(meta, cos_full, sin_full, owns, terms):
    slots, width = terms[0].shape
    grad = jax.ShapeDtypeStruct((slots, width // 2), jnp.bfloat16)
    return pl.pallas_call(
        functools.partial(finish_kernel, len(terms) + 1),
        out_shape=(grad, grad),
        in_specs=[SMEM] + [VMEM] * (2 + len(owns) + len(terms)),
        out_specs=(VMEM, VMEM),
        compiler_params=vmem(0, 16, 16),
        name="finish",
    )(meta, cos_full, sin_full, *terms, *owns)


def part_of(part, size):
    return slice(part * size, (part + 1) * size)


def spread(sent, sent_again, turned_keys, values, ctx_size):
    if relayed(ctx_size):
        alpha = [lax.ppermute(part, "ctx", [(0, 2), (2, 3)]) for part in (turned_keys, values)]
        beta = lax.ppermute(sent, "ctx", [(1, 3)])
        gamma = lax.ppermute(sent_again, "ctx", [(0, 1), (1, 2)])
        delta = [lax.ppermute(part, "ctx", [(2, 3)]) for part in alpha]
        return [*alpha, beta, gamma, *delta]
    blocks = [sent]
    for hop in range(1, ctx_size):
        pairs = [(shard, shard + 1) for shard in range(hop - 1, ctx_size - 1)]
        blocks.append(lax.ppermute(blocks[-1], "ctx", pairs))
    return blocks[1:]


def relay_first(first, third):
    first = lax.ppermute(first, "ctx", [(3, 2), (2, 1), (1, 0)])
    third = (third + first.astype(jnp.float32)).astype(jnp.bfloat16)
    return [first, lax.ppermute(third, "ctx", [(3, 2), (2, 0)])]


def descend(terms, ctx_size):
    arrived = []
    for hop, term in enumerate(terms, 1):
        pairs = [(shard + hop, shard) for shard in range(ctx_size - hop)]
        arrived.append(lax.ppermute(term, "ctx", pairs))
    return arrived


def body(positions, queries, keys, values, out_grad):
    ctx_size = lax.axis_size("ctx")
    routed = positions.shape[1]
    meta, cos_full, sin_full, sent, turned_keys = prepare(positions, keys[0], values[0], ctx_size)
    turned, turned_t, grad_t, sent_again = rotate_queries(
        cos_full, sin_full, queries[0], out_grad[0], sent
    )
    blocks = spread(sent, sent_again, turned_keys, values[0], ctx_size)
    own = own_scores(sent, turned_t, grad_t)
    key_heads = keys.shape[2] // HEAD_DIM
    parts = 1 if routed <= 512 else key_heads
    wide, narrow = queries.shape[2] // parts, sent.shape[1] // parts
    terms, joined = [], []
    for part in range(parts):
        columns = part_of(part, wide)
        outs = scores(
            meta,
            turned[:, columns],
            out_grad[0][:, columns],
            turned_t[columns],
            grad_t[columns],
            own[2][part_of(part, wide // HEAD_DIM)],
            [block[:, part_of(part, narrow)] for block in blocks],
            routed,
            ctx_size,
        )
        terms.append(outs[0])
        joined.append(outs[1])
    terms = [jnp.concatenate(term, axis=1) for term in zip(*terms)]
    if relayed(ctx_size):
        arrived, later = relay_first(terms[0], terms[2]), [terms[1]]
    else:
        arrived, later = descend(terms, ctx_size), []
    dqs, owns = [], []
    for key_head in range(key_heads):
        call, part = (0, key_head) if parts == 1 else (key_head, 0)
        dq, own_terms, *later = local_terms(
            part,
            key_head,
            meta,
            cos_full,
            sin_full,
            turned,
            out_grad[0],
            sent,
            own,
            joined[call],
            later,
        )
        dqs.append(dq)
        owns.append(own_terms)
        for term in later:
            arrived.append(lax.ppermute(term, "ctx", [(3, 1)]))
        later = []
    dq = jnp.concatenate(dqs, axis=1)
    key_grad, value_grad = finish(meta, cos_full, sin_full, owns, arrived)
    return (dq[None], key_grad[None], value_grad[None])


def solution(mesh):
    split = P(("groups", "dp"), "ctx", "mp")
    return jax.shard_map(
        body,
        mesh=mesh,
        in_specs=(P(("groups", "dp"), None), split, split, split, split),
        out_specs=(split, split, split),
        check_vma=False,
    )
```

profile of v0, /device:TPU:0, one launch (start us, length us, event | category | flops | bytes accessed | tf_op | source)
XLA Modules:
  0.0 58.0 jit_solution(1559647192161522556)
XLA Ops:
  0.6 5.9 %collective-permute-start.1 = (bf16[256,256]{1,0:T(8,128)(2,1)}, bf16[256,256]{1,0:T(8,128)(2,1)S(1)}, u32[]{:S(2)}, u32[]{:S(2)}) collective-permute-start(bf16[256,256]{1,0:T(8,128)(2,1)} %bitcast.14), channel_id=1, source_target_pairs={{0,8},{8,12},{1,9},{9,13},{2,10},{10,14},{3,11},{11,15},{16,24},{2... | collective-permute-start | bytes 393224 | tf_op jit(solution)/shard_map/ppermute | solution.py:547
  6.6 2.3 %prepare.1 = (s32[8]{0:T(128)}, f32[256,128]{1,0:T(8,128)}, f32[256,128]{1,0:T(8,128)}, bf16[256,512]{1,0:T(8,128)(2,1)}, bf16[256,256]{1,0:T(8,128)(2,1)}) custom-call(f32[2,128]{1,0:T(2,128)} %constant.2.clone.rows_hbm, s32[1,512]{1,0:T(1,128)} %pos_hbm.1, bf16[256,256]{1,0:T(8,128)(2,1)} %bitcast.13, bf16[256,256]{1,0:T(8,128)(2,1)} %bitcast.15), custom_call_target="tpu_custom_call" | custom-call | tf_op jit(solution)/shard_map/prepare/pallas_call | solution.py:115
  8.9 3.5 %collective-permute-start = (bf16[256,256]{1,0:T(8,128)(2,1)}, bf16[256,256]{1,0:T(8,128)(2,1)S(1)}, u32[]{:S(2)}, u32[]{:S(2)}) collective-permute-start(bf16[256,256]{1,0:T(8,128)(2,1)} %get-tuple-element.38), channel_id=1, source_target_pairs={{0,8},{8,12},{1,9},{9,13},{2,10},{10,14},{3,11},{11,15},{16,24},{2... | collective-permute-start | bytes 393224 | tf_op jit(solution)/shard_map/ppermute | solution.py:547
  12.4 0.7 %collective-permute-start.2 = (bf16[256,512]{1,0:T(8,128)(2,1)}, bf16[256,512]{1,0:T(8,128)(2,1)S(1)}, u32[]{:S(2)}, u32[]{:S(2)}) collective-permute-start(bf16[256,512]{1,0:T(8,128)(2,1)} %get-tuple-element.31.sent_ref), channel_id=1, source_target_pairs={{4,12},{5,13},{6,14},{7,15},{20,28},{21,29},{22,30},{23,31}} | collective-permute-start | bytes 786440 | tf_op jit(solution)/shard_map/ppermute | solution.py:548
  13.1 0.0 copy-start
  13.1 1.2 %copy-done = bf16[1,256,2048]{2,1,0:T(8,128)(2,1)S(1)} copy-done((bf16[1,256,2048]{2,1,0:T(8,128)(2,1)S(1)}, bf16[1,256,2048]{2,1,0:T(8,128)(2,1)}, u32[]{:S(2)}) %copy-start) | copy-done | bytes 1048600
  14.3 0.9 %copy-done.2 = f32[256,128]{1,0:T(8,128)S(1)} copy-done((f32[256,128]{1,0:T(8,128)S(1)}, f32[256,128]{1,0:T(8,128)}, u32[]{:S(2)}) %copy-start.2) | copy-done | bytes 131096
  15.2 0.9 %copy-done.4 = f32[256,128]{1,0:T(8,128)S(1)} copy-done((f32[256,128]{1,0:T(8,128)S(1)}, f32[256,128]{1,0:T(8,128)}, u32[]{:S(2)}) %copy-start.4) | copy-done | bytes 131096
  16.1 0.9 %copy-done.6 = bf16[256,512]{1,0:T(8,128)(2,1)S(1)} copy-done((bf16[256,512]{1,0:T(8,128)(2,1)S(1)}, bf16[256,512]{1,0:T(8,128)(2,1)}, u32[]{:S(2)}) %copy-start.6) | copy-done | bytes 262168
  17.1 1.2 %copy-done.9 = bf16[1,256,2048]{2,1,0:T(8,128)(2,1)S(1)} copy-done((bf16[1,256,2048]{2,1,0:T(8,128)(2,1)S(1)}, bf16[1,256,2048]{2,1,0:T(8,128)(2,1)}, u32[]{:S(2)}) %copy-start.9) | copy-done | bytes 1048600
  18.3 1.1 %rotate_queries.1 = (bf16[256,2048]{1,0:T(8,128)(2,1)S(1)}, bf16[2048,256]{1,0:T(8,128)(2,1)S(1)}, bf16[2048,256]{1,0:T(8,128)(2,1)S(1)}, bf16[256,512]{1,0:T(8,128)(2,1)S(1)}) custom-call(f32[256,128]{1,0:T(8,128)S(1)} %copy-done.2, f32[256,128]{1,0:T(8,128)S(1)} %copy-done.4, bf16[256,2048]{1,0:T(8,128)(2,1)S(1)} %bitcast.12, ...), custom_call_target="tpu_custom_call" | custom-call | flops 3000000000 | bytes 4194304 | tf_op jit(solution)/shard_map/rotate_queries/pallas_call | solution.py:157
  19.4 1.9 %collective-permute-start.3 = (bf16[256,512]{1,0:T(8,128)(2,1)S(1)}, bf16[256,512]{1,0:T(8,128)(2,1)S(1)}, u32[]{:S(2)}, u32[]{:S(2)}) collective-permute-start(bf16[256,512]{1,0:T(8,128)(2,1)S(1)} %get-tuple-element.39), channel_id=1, source_target_pairs={{0,4},{4,8},{1,5},{5,9},{2,6},{6,10},{3,7},{7,11},{16,20},{20,24},... | collective-permute-start | bytes 786440 | tf_op jit(solution)/shard_map/ppermute | solution.py:549
  21.4 0.7 %collective-permute-start.5 = (bf16[256,256]{1,0:T(8,128)(2,1)S(1)}, bf16[256,256]{1,0:T(8,128)(2,1)S(1)}, u32[]{:S(2)}, u32[]{:S(2)}) collective-permute-start(bf16[256,256]{1,0:T(8,128)(2,1)S(1)} %collective-permute-done.1.refs_1_), channel_id=1, source_target_pairs={{8,12},{9,13},{10,14},{11,15},{24,28},{25,29},{26,30},{27,31}} | collective-permute-start | bytes 393224 | tf_op jit(solution)/shard_map/ppermute | solution.py:550
  22.1 0.0 collective-permute-done.refs_0_
  22.1 0.7 %collective-permute-start.4 = (bf16[256,256]{1,0:T(8,128)(2,1)S(1)}, bf16[256,256]{1,0:T(8,128)(2,1)S(1)}, u32[]{:S(2)}, u32[]{:S(2)}) collective-permute-start(bf16[256,256]{1,0:T(8,128)(2,1)S(1)} %collective-permute-done.refs_0_), channel_id=1, source_target_pairs={{8,12},{9,13},{10,14},{11,15},{24,28},{25,29},{26,30},{27,31}} | collective-permute-start | bytes 393224 | tf_op jit(solution)/shard_map/ppermute | solution.py:550
  22.8 0.0 copy-start.1
  22.8 2.2 %own_scores.1 = (f32[16,256,256]{2,1,0:T(8,128)S(1)}, f32[16,256,256]{2,1,0:T(8,128)S(1)}, f32[16,8,256]{2,1,0:T(8,128)S(1)}) custom-call(bf16[256,512]{1,0:T(8,128)(2,1)S(1)} %copy-done.7, bf16[2048,256]{1,0:T(8,128)(2,1)S(1)} %get-tuple-element.33.turned_t_ref, bf16[2048,256]{1,0:T(8,128)(2,1)S(1)} %get-tuple-element.34.grad_t_ref), custom_call_target="tpu_custom_call" | custom-call | flops 5000000000 | bytes 10485760 | tf_op jit(solution)/shard_map/own_scores/pallas_call | solution.py:245
  25.0 0.0 collective-permute-done.4.refs_4_
  25.0 0.0 collective-permute-done.2.refs_2_
  25.0 1.6 %collective-permute-done.3.refs_3_ = bf16[256,512]{1,0:T(8,128)(2,1)S(1)} collective-permute-done((bf16[256,512]{1,0:T(8,128)(2,1)S(1)}, bf16[256,512]{1,0:T(8,128)(2,1)S(1)}, u32[]{:S(2)}, u32[]{:S(2)}) %collective-permute-start.3) | collective-permute-done | bytes 262176 | tf_op jit(solution)/shard_map/ppermute | solution.py:549
  26.6 1.2 %scores.1 = (bf16[256,512]{1,0:T(8,128)(2,1)S(1)}, bf16[256,512]{1,0:T(8,128)(2,1)S(1)}, f32[256,512]{1,0:T(8,128)S(1)}, bf16[2,576,2048]{2,1,0:T(8,128)(2,1)S(1...) custom-call(s32[8]{0:T(128)S(1)} %copy-done.8, bf16[256,2048]{1,0:T(8,128)(2,1)S(1)} %get-tuple-element.32.turned_ref, ...), custom_call_target="tpu_custom_call" | custom-call | flops 8000000000 | bytes 12582912 | tf_op jit(solution)/shard_map/scores/pallas_call | solution.py:398
  27.9 1.3 %collective-permute-start.6 = (bf16[256,512]{1,0:T(8,128)(2,1)S(1)}, bf16[256,512]{1,0:T(8,128)(2,1)S(1)}, u32[]{:S(2)}, u32[]{:S(2)}) collective-permute-start(bf16[256,512]{1,0:T(8,128)(2,1)S(1)} %get-tuple-element.46), channel_id=1, source_target_pairs={{12,8},{8,4},{4,0},{13,9},{9,5},{5,1},{14,10},{10,6},{6,2},{15,11}... | collective-permute-start | bytes 786440 | tf_op jit(solution)/shard_map/ppermute | solution.py:560
  29.2 2.0 %local_terms.2 = (bf16[256,1024]{1,0:T(8,128)(2,1)S(1)}, f32[256,256]{1,0:T(8,128)S(1)}, bf16[256,512]{1,0:T(8,128)(2,1)S(1)}) custom-call(s32[8]{0:T(128)S(1)} %copy-done.8, f32[256,128]{1,0:T(8,128)S(1)} %copy-done.3, f32[256,128]{1,0:T(8,128)S(1)} %copy-done.5, bf16[256,2048]{1,0:T(8,128)(2,1)S(1)} %get-tuple-element.32.turned_ref, ...), custom_call_target="tpu_custom_call" | custom-call | flops 4000000000 | bytes 10485760 | tf_op jit(solution)/shard_map/local_terms/pallas_call | solution.py:487
  31.2 0.7 %collective-permute-start.8 = (bf16[256,512]{1,0:T(8,128)(2,1)S(1)}, bf16[256,512]{1,0:T(8,128)(2,1)S(1)}, u32[]{:S(2)}, u32[]{:S(2)}) collective-permute-start(bf16[256,512]{1,0:T(8,128)(2,1)S(1)} %get-tuple-element.48), channel_id=1, source_target_pairs={{12,4},{13,5},{14,6},{15,7},{28,20},{29,21},{30,22},{31,23}} | collective-permute-start | bytes 786440 | tf_op jit(solution)/shard_map/ppermute | solution.py:625
  31.8 12.2 %collective-permute-done.6.refs_0_ = bf16[256,512]{1,0:T(8,128)(2,1)S(1)} collective-permute-done((bf16[256,512]{1,0:T(8,128)(2,1)S(1)}, bf16[256,512]{1,0:T(8,128)(2,1)S(1)}, u32[]{:S(2)}, u32[]{:S(2)}) %collective-permute-start.6) | collective-permute-done | bytes 262176 | tf_op jit(solution)/shard_map/ppermute | solution.py:560
  44.0 0.1 add_convert_fusion
  44.1 1.3 %collective-permute-start.7 = (bf16[256,512]{1,0:T(8,128)(2,1)S(1)}, bf16[256,512]{1,0:T(8,128)(2,1)S(1)}, u32[]{:S(2)}, u32[]{:S(2)}) collective-permute-start(bf16[256,512]{1,0:T(8,128)(2,1)S(1)} %add_convert_fusion), channel_id=1, source_target_pairs={{12,8},{8,0},{13,9},{9,1},{14,10},{10,2},{15,11},{11,3},{28,24},{2... | collective-permute-start | bytes 786440 | tf_op jit(solution)/shard_map/ppermute | solution.py:562
  45.4 2.0 %local_terms.3 = (bf16[256,1024]{1,0:T(8,128)(2,1)S(1)}, f32[256,256]{1,0:T(8,128)S(1)}) custom-call(s32[8]{0:T(128)S(1)} %copy-done.8, f32[256,128]{1,0:T(8,128)S(1)} %copy-done.3, f32[256,128]{1,0:T(8,128)S(1)} %copy-done.5, bf16[256,2048]{1,0:T(8,128)(2,1)S(1)} %get-tuple-element.32.turned_ref, bf16[256,2048]{1,0:T(8,128)(2,1)S(1)} %bitcast.11, ...), custom_call_target="tpu_custom_call" | custom-call | flops 4000000000 | bytes 10485760 | tf_op jit(solution)/shard_map/local_terms/pallas_call | solution.py:487
  47.4 1.1 %maximum_bitcast_fusion = bf16[1,256,2048]{2,1,0:T(8,128)(2,1)} fusion(bf16[256,1024]{1,0:T(8,128)(2,1)S(1)} %get-tuple-element.45, bf16[256,1024]{1,0:T(8,128)(2,1)S(1)} %get-tuple-element.44), kind=kLoop, calls=%fused_computation | loop fusion | flops 2097152 | bytes 2097152 | tf_op jit(solution)/shard_map/broadcast_in_dim | solution.py:629
  48.4 0.0 collective-permute-done.8.refs_2_
  48.4 8.1 %collective-permute-done.7.refs_1_ = bf16[256,512]{1,0:T(8,128)(2,1)S(1)} collective-permute-done((bf16[256,512]{1,0:T(8,128)(2,1)S(1)}, bf16[256,512]{1,0:T(8,128)(2,1)S(1)}, u32[]{:S(2)}, u32[]{:S(2)}) %collective-permute-start.7) | collective-permute-done | bytes 262176 | tf_op jit(solution)/shard_map/ppermute | solution.py:562
  56.6 1.4 %finish.1 = (bf16[256,256]{1,0:T(8,128)(2,1)}, bf16[256,256]{1,0:T(8,128)(2,1)}) custom-call(s32[8]{0:T(128)S(1)} %copy-done.8, f32[256,128]{1,0:T(8,128)S(1)} %copy-done.3, f32[256,128]{1,0:T(8,128)S(1)} %copy-done.5, bf16[256,512]{1,0:T(8,128)(2,1)S(1)} %collective-permute-done.6.refs_0_, bf16[256,512]{1,0:T(8,128)(2,1)S(1)} %collective-permute-done.7.refs_1_, ...), custom_call_target="tpu_custom_call" | custom-call | tf_op jit(solution)/shard_map/finish/pallas_call | solution.py:531
  (15 shorter events, 0.0 us)
Async XLA Ops:
  0.6 20.7 %collective-permute-start.1 = (bf16[256,256]{1,0:T(8,128)(2,1)}, bf16[256,256]{1,0:T(8,128)(2,1)S(1)}, u32[]{:S(2)}, u32[]{:S(2)}) collective-permute-start(bf16[256,256]{1,0:T(8,128)(2,1)} %bitcast.14), channel_id=1, source_target_pairs={{0,8},{8,12},{1,9},{9,13},{2,10},{10,14},{3,11},{11,15},{16,24},{2... | collective-permute-start | bytes 393224 | tf_op jit(solution)/shard_map/ppermute | solution.py:547
  8.9 13.2 %collective-permute-start = (bf16[256,256]{1,0:T(8,128)(2,1)}, bf16[256,256]{1,0:T(8,128)(2,1)S(1)}, u32[]{:S(2)}, u32[]{:S(2)}) collective-permute-start(bf16[256,256]{1,0:T(8,128)(2,1)} %get-tuple-element.38), channel_id=1, source_target_pairs={{0,8},{8,12},{1,9},{9,13},{2,10},{10,14},{3,11},{11,15},{16,24},{2... | collective-permute-start | bytes 393224 | tf_op jit(solution)/shard_map/ppermute | solution.py:547
  12.4 12.6 %collective-permute-start.2 = (bf16[256,512]{1,0:T(8,128)(2,1)}, bf16[256,512]{1,0:T(8,128)(2,1)S(1)}, u32[]{:S(2)}, u32[]{:S(2)}) collective-permute-start(bf16[256,512]{1,0:T(8,128)(2,1)} %get-tuple-element.31.sent_ref), channel_id=1, source_target_pairs={{4,12},{5,13},{6,14},{7,15},{20,28},{21,29},{22,30},{23,31}} | collective-permute-start | bytes 786440 | tf_op jit(solution)/shard_map/ppermute | solution.py:548
  13.1 1.2 %copy-start = (bf16[1,256,2048]{2,1,0:T(8,128)(2,1)S(1)}, bf16[1,256,2048]{2,1,0:T(8,128)(2,1)}, u32[]{:S(2)}) copy-start(bf16[1,256,2048]{2,1,0:T(8,128)(2,1)} %param.10) | copy-start | bytes 3145732
  14.3 0.9 %copy-start.2 = (f32[256,128]{1,0:T(8,128)S(1)}, f32[256,128]{1,0:T(8,128)}, u32[]{:S(2)}) copy-start(f32[256,128]{1,0:T(8,128)} %get-tuple-element.29.cos_ref) | copy-start | bytes 393220
  15.2 0.9 %copy-start.4 = (f32[256,128]{1,0:T(8,128)S(1)}, f32[256,128]{1,0:T(8,128)}, u32[]{:S(2)}) copy-start(f32[256,128]{1,0:T(8,128)} %get-tuple-element.30.sin_ref) | copy-start | bytes 393220
  16.1 0.9 %copy-start.6 = (bf16[256,512]{1,0:T(8,128)(2,1)S(1)}, bf16[256,512]{1,0:T(8,128)(2,1)}, u32[]{:S(2)}) copy-start(bf16[256,512]{1,0:T(8,128)(2,1)} %get-tuple-element.31.sent_ref) | copy-start | bytes 786436
  17.1 1.2 %copy-start.9 = (bf16[1,256,2048]{2,1,0:T(8,128)(2,1)S(1)}, bf16[1,256,2048]{2,1,0:T(8,128)(2,1)}, u32[]{:S(2)}) copy-start(bf16[1,256,2048]{2,1,0:T(8,128)(2,1)} %param.7) | copy-start | bytes 3145732
  18.3 4.5 %copy-start.7 = (bf16[256,512]{1,0:T(8,128)(2,1)S(1)}, bf16[256,512]{1,0:T(8,128)(2,1)}, u32[]{:S(2)}) copy-start(bf16[256,512]{1,0:T(8,128)(2,1)} %get-tuple-element.31.sent_ref) | copy-start | bytes 786436
  19.4 7.2 %collective-permute-start.3 = (bf16[256,512]{1,0:T(8,128)(2,1)S(1)}, bf16[256,512]{1,0:T(8,128)(2,1)S(1)}, u32[]{:S(2)}, u32[]{:S(2)}) collective-permute-start(bf16[256,512]{1,0:T(8,128)(2,1)S(1)} %get-tuple-element.39), channel_id=1, source_target_pairs={{0,4},{4,8},{1,5},{5,9},{2,6},{6,10},{3,7},{7,11},{16,20},{20,24},... | collective-permute-start | bytes 786440 | tf_op jit(solution)/shard_map/ppermute | solution.py:549
  21.4 3.6 %collective-permute-start.5 = (bf16[256,256]{1,0:T(8,128)(2,1)S(1)}, bf16[256,256]{1,0:T(8,128)(2,1)S(1)}, u32[]{:S(2)}, u32[]{:S(2)}) collective-permute-start(bf16[256,256]{1,0:T(8,128)(2,1)S(1)} %collective-permute-done.1.refs_1_), channel_id=1, source_target_pairs={{8,12},{9,13},{10,14},{11,15},{24,28},{25,29},{26,30},{27,31}} | collective-permute-start | bytes 393224 | tf_op jit(solution)/shard_map/ppermute | solution.py:550
  22.1 2.9 %collective-permute-start.4 = (bf16[256,256]{1,0:T(8,128)(2,1)S(1)}, bf16[256,256]{1,0:T(8,128)(2,1)S(1)}, u32[]{:S(2)}, u32[]{:S(2)}) collective-permute-start(bf16[256,256]{1,0:T(8,128)(2,1)S(1)} %collective-permute-done.refs_0_), channel_id=1, source_target_pairs={{8,12},{9,13},{10,14},{11,15},{24,28},{25,29},{26,30},{27,31}} | collective-permute-start | bytes 393224 | tf_op jit(solution)/shard_map/ppermute | solution.py:550
  22.8 3.9 %copy-start.1 = (bf16[1,256,2048]{2,1,0:T(8,128)(2,1)S(1)}, bf16[1,256,2048]{2,1,0:T(8,128)(2,1)}, u32[]{:S(2)}) copy-start(bf16[1,256,2048]{2,1,0:T(8,128)(2,1)} %param.10) | copy-start | bytes 3145732
  22.8 3.9 %copy-start.8 = (s32[8]{0:T(128)S(1)}, s32[8]{0:T(128)}, u32[]{:S(2)}) copy-start(s32[8]{0:T(128)} %get-tuple-element.28.meta_ref) | copy-start | bytes 100
  26.6 2.5 %copy-start.3 = (f32[256,128]{1,0:T(8,128)S(1)}, f32[256,128]{1,0:T(8,128)}, u32[]{:S(2)}) copy-start(f32[256,128]{1,0:T(8,128)} %get-tuple-element.29.cos_ref) | copy-start | bytes 393220
  26.6 2.5 %copy-start.5 = (f32[256,128]{1,0:T(8,128)S(1)}, f32[256,128]{1,0:T(8,128)}, u32[]{:S(2)}) copy-start(f32[256,128]{1,0:T(8,128)} %get-tuple-element.30.sin_ref) | copy-start | bytes 393220
  27.9 16.2 %collective-permute-start.6 = (bf16[256,512]{1,0:T(8,128)(2,1)S(1)}, bf16[256,512]{1,0:T(8,128)(2,1)S(1)}, u32[]{:S(2)}, u32[]{:S(2)}) collective-permute-start(bf16[256,512]{1,0:T(8,128)(2,1)S(1)} %get-tuple-element.46), channel_id=1, source_target_pairs={{12,8},{8,4},{4,0},{13,9},{9,5},{5,1},{14,10},{10,6},{6,2},{15,11}... | collective-permute-start | bytes 786440 | tf_op jit(solution)/shard_map/ppermute | solution.py:560
  31.2 17.3 %collective-permute-start.8 = (bf16[256,512]{1,0:T(8,128)(2,1)S(1)}, bf16[256,512]{1,0:T(8,128)(2,1)S(1)}, u32[]{:S(2)}, u32[]{:S(2)}) collective-permute-start(bf16[256,512]{1,0:T(8,128)(2,1)S(1)} %get-tuple-element.48), channel_id=1, source_target_pairs={{12,4},{13,5},{14,6},{15,7},{28,20},{29,21},{30,22},{31,23}} | collective-permute-start | bytes 786440 | tf_op jit(solution)/shard_map/ppermute | solution.py:625
  44.1 12.4 %collective-permute-start.7 = (bf16[256,512]{1,0:T(8,128)(2,1)S(1)}, bf16[256,512]{1,0:T(8,128)(2,1)S(1)}, u32[]{:S(2)}, u32[]{:S(2)}) collective-permute-start(bf16[256,512]{1,0:T(8,128)(2,1)S(1)} %add_convert_fusion), channel_id=1, source_target_pairs={{12,8},{8,0},{13,9},{9,1},{14,10},{10,2},{15,11},{11,3},{28,24},{2... | collective-permute-start | bytes 786440 | tf_op jit(solution)/shard_map/ppermute | solution.py:562
where the time goes:
time: 58.4 us; the launch traced here: 58 us
  waiting for transfers between devices  21.9 us (38%)
  starting transfers between devices  16.6 us (28%)
  Pallas kernels  12.2 us (21%)
  local copies, waits for them, and re-layouts  5.22 us (9%)
  other arithmetic  1.13 us (2%)
  between operations  0.85 us (1%)
    ppermute x1, waiting for transfers between devices, relay_first(): first = lax.ppermute(first, 'ctx', [(3, 2), (2, 1), (1, 0)])  12.2 us
    ppermute x2, starting transfers between devices, spread(): lax.ppermute(part, 'ctx', [(0, 2), (2, 3)])  9.43 us
    ppermute x1, waiting for transfers between devices, relay_first(): return [first, lax.ppermute(third, 'ctx', [(3, 2), (2, 0)])]  8.13 us
    unnamed x20, local copies, waits for them, and re-layouts  5.22 us
    pallas_call x2, Pallas kernels, local_terms(): pl.pallas_call(functools.partial(local_kernel, part, key_head), out_shape...  3.92 us
    pallas_call x1, Pallas kernels, prepare(): pl.pallas_call(functools.partial(prepare_kernel, ctx_size), out_shape=(ja...  2.31 us
    pallas_call x1, Pallas kernels, own_scores(): pl.pallas_call(functools.partial(own_kernel, 4), out_shape=(square, squar...  2.21 us
    ppermute x1, starting transfers between devices, spread(): gamma = lax.ppermute(sent_again, 'ctx', [(0, 1), (1, 2)])  1.93 us
  transfers between devices with their start and end apart: 9, of which 3 were waited for; matrix products, arithmetic and copies ran while one was open for 2% of the time, Pallas kernels for 17%

commit v1 on v0

--- a/solution.py
+++ b/solution.py
@@ -22,7 +22,6 @@
 
 VMEM = pl.BlockSpec(memory_space=pltpu.VMEM)
 SMEM = pl.BlockSpec(memory_space=pltpu.SMEM)
-HBM = pl.BlockSpec(memory_space=pltpu.HBM)
 
 
 def vmem(routed, small, large):
@@ -41,12 +40,15 @@
     return field * cos_full - pltpu.roll(field, HALF_DIM, 1) * sin_full
 
 
-def rope_rows():
+def frequencies():
     ladder = np.arange(HALF_DIM, dtype=np.float32)
     exponent = ladder * np.float32(-2.0 * math.log(ROPE_BASE) / HEAD_DIM)
     freq = np.exp(exponent.astype(np.float64)).astype(np.float32)
-    sign = np.repeat(np.array([-1.0, 1.0], np.float32), HALF_DIM)
-    return np.stack([np.concatenate([freq, freq]), sign])
+    entry = lax.broadcasted_iota(jnp.int32, (1, HEAD_DIM), 1) % HALF_DIM
+    row = jnp.zeros((1, HEAD_DIM), jnp.float32)
+    for index in range(HALF_DIM):
+        row = jnp.where(entry == index, float(freq[index]), row)
+    return row
 
 
 def shard_layout(ctx_size, me, pos, meta_ref):
@@ -71,32 +73,20 @@
 
 
 def prepare_kernel(
-    ctx_size, rows_hbm, pos_hbm, keys_hbm, values_hbm, meta_ref, cos_ref, sin_ref, sent_ref, turned_ref, *refs
+    ctx_size, pos_ref, keys_ref, values_ref, meta_ref, cos_ref, sin_ref, sent_ref, turned_ref
 ):
-    rows_ref, pos_ref, keys_ref, values_ref, sems = refs
-    sources = (pos_hbm, rows_hbm, keys_hbm, values_hbm)
-    targets = (pos_ref, rows_ref, keys_ref, values_ref)
-    copies = [
-        pltpu.make_async_copy(source, target, sems.at[index])
-        for index, (source, target) in enumerate(zip(sources, targets))
-    ]
-    for copy in copies:
-        copy.start()
-    copies[0].wait()
     slots = keys_ref.shape[0]
     pos = pos_ref[...]
     my_first = shard_layout(ctx_size, lax.axis_index("ctx"), pos, meta_ref)
     shape = (slots, pos.shape[1])
     gap = lax.broadcasted_iota(jnp.int32, shape, 1) - lax.broadcasted_iota(jnp.int32, shape, 0)
     named = jnp.where(gap == my_first, pos.astype(jnp.float32), 0.0)
-    copies[1].wait()
-    angles = jnp.sum(named, axis=1, keepdims=True) * rows_ref[0:1, :]
+    angles = jnp.sum(named, axis=1, keepdims=True) * frequencies()
     cos_full = jnp.cos(angles)
-    sin_full = jnp.sin(angles) * rows_ref[1:2, :]
+    front = lax.broadcasted_iota(jnp.int32, angles.shape, 1) < HALF_DIM
+    sin_full = jnp.where(front, -jnp.sin(angles), jnp.sin(angles))
     cos_ref[...] = cos_full
     sin_ref[...] = sin_full
-    copies[2].wait()
-    copies[3].wait()
     for lane in range(0, keys_ref.shape[1], HEAD_DIM):
         lanes = slice(lane, lane + HEAD_DIM)
         key = turn(keys_ref[:, lanes].astype(jnp.float32), cos_full, sin_full)
@@ -108,10 +98,8 @@
 
 def prepare(positions, keys, values, ctx_size):
     slots, width = keys.shape
-    rows = jnp.asarray(rope_rows())
     table = jax.ShapeDtypeStruct((slots, HEAD_DIM), jnp.float32)
     sent = jax.ShapeDtypeStruct((slots, 2 * width), jnp.bfloat16)
-    operands = (rows, positions, keys, values)
     return pl.pallas_call(
         functools.partial(prepare_kernel, ctx_size),
         out_shape=(
@@ -121,27 +109,15 @@
             sent,
             jax.ShapeDtypeStruct((slots, width), jnp.bfloat16),
         ),
-        in_specs=[HBM] * 4,
+        in_specs=[VMEM] * 3,
         out_specs=(SMEM, VMEM, VMEM, VMEM, VMEM),
-        scratch_shapes=[pltpu.VMEM(operand.shape, operand.dtype) for operand in operands]
-        + [pltpu.SemaphoreType.DMA((4,))],
-        compiler_params=vmem(positions.shape[1], 60, 60),
+        compiler_params=vmem(positions.shape[1], 16, 32),
         name="prepare",
-    )(*operands)
-
-
-def queries_kernel(
-    cos_ref,
-    sin_ref,
-    query_ref,
-    grad_ref,
-    sent_ref,
-    turned_ref,
-    turned_t_ref,
-    grad_t_ref,
-    sent_again_ref,
-):
-    sent_again_ref[...] = sent_ref[...]
+    )(positions, keys, values)
+
+
+def queries_kernel(cos_ref, sin_ref, query_ref, grad_ref, *refs):
+    turned_ref, turned_t_ref, grad_t_ref = refs[-3:]
     for lane in range(0, query_ref.shape[1], HEAD_DIM):
         lanes = slice(lane, lane + HEAD_DIM)
         query = turn(query_ref[:, lanes].astype(jnp.float32), cos_ref[...], sin_ref[...])
@@ -150,21 +126,21 @@
         grad_t_ref[lanes, :] = grad_ref[:, lanes].astype(jnp.float32).T.astype(jnp.bfloat16)
 
 
-def rotate_queries(cos_full, sin_full, queries, out_grad, sent):
+def rotate_queries(cos_full, sin_full, queries, out_grad, after):
     slots, width = queries.shape
     straight = jax.ShapeDtypeStruct((slots, width), jnp.bfloat16)
     across = jax.ShapeDtypeStruct((width, slots), jnp.bfloat16)
     return pl.pallas_call(
         queries_kernel,
-        out_shape=(straight, across, across, jax.ShapeDtypeStruct(sent.shape, sent.dtype)),
+        out_shape=(straight, across, across),
         in_specs=[VMEM] * 5,
-        out_specs=(VMEM,) * 4,
+        out_specs=(VMEM,) * 3,
         compiler_params=vmem(0, 16, 16),
         cost_estimate=pl.CostEstimate(
             flops=3 * 10**9, bytes_accessed=4 * 1024 * 1024, transcendentals=0
         ),
         name="rotate_queries",
-    )(cos_full, sin_full, queries, out_grad, sent)
+    )(cos_full, sin_full, queries, out_grad, after)
 
 
 def stacked(ref, lane, heads, width):
@@ -172,11 +148,11 @@
     return jnp.concatenate(parts, axis=0)
 
 
-def beside(ref, rows, slots, width):
+def beside(ref, rows, column, heads, slots, width):
     if width == slots:
-        return ref[:rows, :]
-    parts = [ref[:rows, lane : lane + width] for lane in range(0, ref.shape[1], slots)]
-    return jnp.concatenate(parts, axis=1)
+        return ref[:rows, column : column + heads * slots]
+    columns = [column + head * slots for head in range(heads)]
+    return jnp.concatenate([ref[:rows, start : start + width] for start in columns], axis=1)
 
 
 def woven(keys, values):
@@ -259,7 +235,7 @@
 def scores_kernel(
     ctx_size,
     sizes,
-    step_heads,
+    step_units,
     meta_ref,
     turned_ref,
     grad_ref,
@@ -301,81 +277,87 @@
     bias_ref[...] = jnp.where(seen, 0.0, HIDDEN)
     live = lax.broadcasted_iota(jnp.int32, (1, slots), 1) < my_count
 
-    def one_head(key_head, head, rows, width):
-        place = key_head * heads + head
-        lanes = pl.ds(pl.multiple_of(place * HEAD_DIM, HEAD_DIM), HEAD_DIM)
-        columns = pl.ds(pl.multiple_of(head * slots, slots), width)
-        bias = jnp.concatenate([bias_ref[:rows, :]] * (width // HEAD_DIM), axis=1)
-        scores = dot(
-            key_ref[:rows, head_lanes(key_head)], turned_t_ref[lanes, :width], ((1,), (0,))
-        )
-        scores = scores + bias
-        prob_grad = dot(
-            value_ref[:rows, head_lanes(key_head)], grad_t_ref[lanes, :width], ((1,), (0,))
-        )
-        own_peak = sums_ref[place, 0:1, :width]
+    def unit(places, rows, width):
+        def joint(ref, index):
+            return jnp.concatenate([ref[index(place)] for place in places], axis=1)
+
+        def head_rows(place):
+            row = pl.multiple_of(place * HEAD_DIM, HEAD_DIM)
+            return (pl.ds(row, HEAD_DIM), slice(0, width))
+
+        def sum_row(row):
+            return joint(sums_ref, lambda place: (place, slice(row, row + 1), slice(0, width)))
+
+        lane = pl.multiple_of(places[0] // heads * HEAD_DIM, HEAD_DIM)
+        lanes = pl.ds(lane, HEAD_DIM)
+        bias = jnp.concatenate([bias_ref[:rows, :]] * (len(places) * width // HEAD_DIM), axis=1)
+        scores = dot(key_ref[:rows, lanes], joint(turned_t_ref, head_rows), ((1,), (0,))) + bias
+        prob_grad = dot(value_ref[:rows, lanes], joint(grad_t_ref, head_rows), ((1,), (0,)))
+        own_peak = sum_row(0)
         peak = jnp.maximum(own_peak, fold(scores, jnp.maximum, jnp.max))
         share = jnp.exp2((own_peak - peak) * EXP2_SCALE)
         weights = jnp.exp2((scores - peak) * EXP2_SCALE)
-        total = sums_ref[place, 1:2, :width] * share + fold(weights, jnp.add, jnp.sum)
-        inverse = 1.0 / total
-        product = sums_ref[place, 2:3, :width] * share
-        delta = (product + fold(weights * prob_grad, jnp.add, jnp.sum)) * inverse
-        inverse = jnp.where(live[:, :width], inverse, 0.0)
-        joined_ref[place, 0:1, :width] = share * inverse
-        joined_ref[place, 1:2, :width] = delta
+        inverse = 1.0 / (sum_row(1) * share + fold(weights, jnp.add, jnp.sum))
+        delta = (sum_row(2) * share + fold(weights * prob_grad, jnp.add, jnp.sum)) * inverse
+        inverse = jnp.where(jnp.concatenate([live[:, :width]] * len(places), axis=1), inverse, 0.0)
+        factor = share * inverse
         prob = weights * inverse
-        prob_ref[:rows, columns] = prob.astype(jnp.bfloat16)
         score_grad = (prob * (prob_grad - delta)).astype(jnp.bfloat16)
-        score_grad_ref[key_head, :rows, columns] = score_grad
-        if width < slots:
-            rest = pl.ds(pl.multiple_of(head * slots + width, HEAD_DIM), slots - width)
-            none = jnp.zeros((rows, slots - width), jnp.bfloat16)
-            score_grad_ref[key_head, :rows, rest] = none
-            joined_ref[place, 0:2, width:] = jnp.zeros((2, slots - width), jnp.float32)
-
-    for key_head in range(key_heads):
-        above = 0
-        for rows, width in sizes:
-            fits = (my_start > above) & (my_start <= rows)
+        prob = prob.astype(jnp.bfloat16)
+        for index, place in enumerate(places):
+            part = slice(index * width, (index + 1) * width)
+            columns = pl.ds(pl.multiple_of(place * slots, slots), width)
+            prob_ref[:rows, columns] = prob[:, part]
+            score_grad_ref[:rows, columns] = score_grad[:, part]
+            joined_ref[place, 0:1, :width] = factor[:, part]
+            joined_ref[place, 1:2, :width] = delta[:, part]
             if width < slots:
-                fits = (my_start > 0) & (my_count <= width)
-            elif any(size[1] < slots for size in sizes):
-                fits = fits & (my_count > sizes[-1][1])
-
-            @pl.when(fits)
-            def _():
-                def step(index, carry):
-                    for part in range(step_heads):
-                        one_head(key_head, index * step_heads + part, rows, width)
-                    return carry
-
-                lax.fori_loop(0, heads // step_heads, step, 0)
-                if rows % CHUNK:
-                    beyond = slice(rows, rows + CHUNK - rows % CHUNK)
-                    none = jnp.zeros((CHUNK - rows % CHUNK, heads * slots), jnp.bfloat16)
-                    score_grad_ref[key_head, beyond, :] = none
-                lane = key_head * heads * HEAD_DIM
-                acc_ref[:rows, :] = terms_of(
-                    beside(prob_ref, rows, slots, width),
-                    beside(score_grad_ref.at[key_head], rows, slots, width),
+                rest = pl.ds(pl.multiple_of(place * slots + width, HEAD_DIM), slots - width)
+                score_grad_ref[:rows, rest] = jnp.zeros((rows, slots - width), jnp.bfloat16)
+                joined_ref[place, 0:2, width:] = jnp.zeros((2, slots - width), jnp.float32)
+
+    all_heads = key_heads * heads
+    above = {}
+    for rows, width in sizes:
+        fits = (my_start > above.get(width, 0)) & (my_start <= rows)
+        above[width] = rows
+        if len(sizes) > 1:
+            fits = fits & ((my_count > slots // 2) if width == slots else (my_count <= width))
+
+        @pl.when(fits)
+        def _():
+            side = slots // width
+
+            def step(index, carry):
+                for part in range(step_units):
+                    place = (index * step_units + part) * side
+                    unit([place + item for item in range(side)], rows, width)
+                return carry
+
+            lax.fori_loop(0, all_heads // side // step_units, step, 0)
+            if rows % CHUNK:
+                beyond = slice(rows, rows + CHUNK - rows % CHUNK)
+                none = jnp.zeros((CHUNK - rows % CHUNK, all_heads * slots), jnp.bfloat16)
+                score_grad_ref[beyond, :] = none
+            for key_head in range(key_heads):
+                lane, column = key_head * heads * HEAD_DIM, key_head * heads * slots
+                acc_ref[:rows, 2 * key_head * HEAD_DIM : 2 * (key_head + 1) * HEAD_DIM] = terms_of(
+                    beside(prob_ref, rows, column, heads, slots, width),
+                    beside(score_grad_ref, rows, column, heads, slots, width),
                     stacked(turned_ref, lane, heads, width),
                     stacked(grad_ref, lane, heads, width),
                 )
 
-            above = rows if width == slots else above
-
-        @pl.when(my_start == 0)
-        def _():
-            for place in range(key_head * heads, (key_head + 1) * heads):
-                inverse = 1.0 / sums_ref[place, 1:2, :]
-                joined_ref[place, 0:1, :] = jnp.where(live, inverse, 0.0)
-                joined_ref[place, 1:2, :] = sums_ref[place, 2:3, :] * inverse
-
-        for hop, term_ref in zip(sent_hops, terms):
-            start = pl.multiple_of(meta_ref[hop], ALIGN)
-            term = acc_ref[pl.ds(start, slots), :].astype(term_ref.dtype)
-            term_ref[:, 2 * key_head * HEAD_DIM : 2 * (key_head + 1) * HEAD_DIM] = term
+    @pl.when(my_start == 0)
+    def _():
+        for place in range(all_heads):
+            inverse = 1.0 / sums_ref[place, 1:2, :]
+            joined_ref[place, 0:1, :] = jnp.where(live, inverse, 0.0)
+            joined_ref[place, 1:2, :] = sums_ref[place, 2:3, :] * inverse
+
+    for hop, term_ref in zip(sent_hops, terms):
+        start = pl.multiple_of(meta_ref[hop], ALIGN)
+        term_ref[...] = acc_ref[pl.ds(start, slots), :].astype(term_ref.dtype)
 
 
 def relayed(ctx_size):
@@ -389,17 +371,18 @@
     key_heads = width // HEAD_DIM // 2
     heads = turned.shape[1] // HEAD_DIM // key_heads
     span = -(-(routed + ctx_size * ALIGN) // CHUNK) * CHUNK
-    sizes, step_heads = [(span, slots)], 1
+    sizes, step_units = [(span, slots)], 1
     if span == 2 * CHUNK and routed - slots // 2 + ctx_size * ALIGN <= 3 * CHUNK // 2 + ALIGN:
-        sizes, step_heads = [(CHUNK, slots), (3 * CHUNK // 2, slots), (span, slots // 2)], 4
+        sizes = [(CHUNK, slots), (3 * CHUNK // 2, slots), (CHUNK, slots // 2), (span, slots // 2)]
+        step_units = 2
     terms = [jax.ShapeDtypeStruct((slots, width), jnp.bfloat16)] * (ctx_size - 1)
     if relayed(ctx_size):
         terms[2] = jax.ShapeDtypeStruct((slots, width), jnp.float32)
     outs = pl.pallas_call(
-        functools.partial(scores_kernel, ctx_size, sizes, step_heads),
+        functools.partial(scores_kernel, ctx_size, sizes, step_units),
         out_shape=(
             *terms,
-            jax.ShapeDtypeStruct((key_heads, span, heads * slots), jnp.bfloat16),
+            jax.ShapeDtypeStruct((span, key_heads * heads * slots), jnp.bfloat16),
             jax.ShapeDtypeStruct((key_heads * heads, 8, slots), jnp.float32),
             jax.ShapeDtypeStruct((span + slots, key_heads * HEAD_DIM), jnp.bfloat16),
         ),
@@ -408,10 +391,10 @@
         scratch_shapes=[
             pltpu.VMEM((span + slots, width // 2), jnp.bfloat16),
             pltpu.VMEM((span, HEAD_DIM), jnp.float32),
-            pltpu.VMEM((span, heads * slots), jnp.bfloat16),
-            pltpu.VMEM((span + slots, 2 * HEAD_DIM), jnp.float32),
+            pltpu.VMEM((span, key_heads * heads * slots), jnp.bfloat16),
+            pltpu.VMEM((span + slots, width), jnp.float32),
         ],
-        compiler_params=vmem(routed, 28, 60),
+        compiler_params=vmem(routed, 18, 60),
         cost_estimate=pl.CostEstimate(
             flops=8 * 10**9, bytes_accessed=12 * 1024 * 1024, transcendentals=0
         ),
@@ -443,7 +426,7 @@
         refs[later + 2 + index][...] = refs[index][...]
     slots = turned_ref.shape[0]
     heads = prob_ref.shape[1] // slots
-    span = score_grad_ref.shape[1]
+    span = score_grad_ref.shape[0]
     my_start = meta_ref[0]
     own_key_t = sent_ref[:, key_lanes(key_head)].astype(jnp.float32).T.astype(jnp.bfloat16)
     for head in range(heads):
@@ -462,8 +445,9 @@
             rows = slice(chunk, chunk + CHUNK)
             key_t = key_ref[rows, head_lanes(part)].astype(jnp.float32).T.astype(jnp.bfloat16)
             for head in range(heads):
-                columns = slice(head * slots, (head + 1) * slots)
-                sum_ref[head] += dot(key_t, score_grad_ref[part, rows, columns], ((1,), (0,)))
+                place = part * heads + head
+                score_grad = score_grad_ref[rows, place * slots : (place + 1) * slots]
+                sum_ref[head] += dot(key_t, score_grad, ((1,), (0,)))
 
     lane = key_head * heads * HEAD_DIM
     for head in range(heads):
@@ -498,7 +482,7 @@
             pltpu.VMEM((slots, heads * slots), jnp.bfloat16),
             pltpu.VMEM((heads, HEAD_DIM, slots), jnp.float32),
         ],
-        compiler_params=vmem(joined[0].shape[1] // 2, 16, 48),
+        compiler_params=vmem(joined[0].shape[0] // 2, 16, 48),
         cost_estimate=pl.CostEstimate(
             flops=4 * 10**9, bytes_accessed=10 * 1024 * 1024, transcendentals=0
         ),
@@ -542,11 +526,11 @@
     return slice(part * size, (part + 1) * size)
 
 
-def spread(sent, sent_again, turned_keys, values, ctx_size):
+def spread(sent, turned_keys, values, ctx_size):
     if relayed(ctx_size):
         alpha = [lax.ppermute(part, "ctx", [(0, 2), (2, 3)]) for part in (turned_keys, values)]
         beta = lax.ppermute(sent, "ctx", [(1, 3)])
-        gamma = lax.ppermute(sent_again, "ctx", [(0, 1), (1, 2)])
+        gamma = lax.ppermute(sent + 0 * alpha[1][:1, :1], "ctx", [(0, 1), (1, 2)])
         delta = [lax.ppermute(part, "ctx", [(2, 3)]) for part in alpha]
         return [*alpha, beta, gamma, *delta]
     blocks = [sent]
@@ -574,10 +558,10 @@
     ctx_size = lax.axis_size("ctx")
     routed = positions.shape[1]
     meta, cos_full, sin_full, sent, turned_keys = prepare(positions, keys[0], values[0], ctx_size)
-    turned, turned_t, grad_t, sent_again = rotate_queries(
-        cos_full, sin_full, queries[0], out_grad[0], sent
+    blocks = spread(sent, turned_keys, values[0], ctx_size)
+    turned, turned_t, grad_t = rotate_queries(
+        cos_full, sin_full, queries[0], out_grad[0], blocks[0]
     )
-    blocks = spread(sent, sent_again, turned_keys, values[0], ctx_size)
     own = own_scores(sent, turned_t, grad_t)
     key_heads = keys.shape[2] // HEAD_DIM
     parts = 1 if routed <= 512 else key_heads

time: 58.4 us -> 61.6 us (1.055); the launches traced: 58 us -> 61.9 us
  waiting for transfers between devices: 21.9 us -> 25.9 us
  Pallas kernels: 12.2 us -> 11 us
  between operations: 0.85 us -> 1.5 us
    ppermute x1, waiting for transfers between devices: 8.13 us -> 15.1 us  [relay_first(): return [first, lax.ppermute(third, 'ctx', [(3, 2), (2, 0)])]]
    ppermute x1, waiting for transfers between devices: 1.6 us -> 0.01 us  [spread(): gamma = lax.ppermute(sent + 0 * alpha[1][:1, :1], 'ctx', [(0, 1), (1, 2)])]
    ppermute x1, waiting for transfers between devices: 12.2 us -> 10.8 us  [relay_first(): first = lax.ppermute(first, 'ctx', [(3, 2), (2, 1), (1, 0)])]
    pallas_call x1, Pallas kernels: 2.31 us -> 1.29 us  [prepare(): pl.pallas_call(functools.partial(prepare_kernel, ctx_size), out_shape=(ja...]
    unnamed x20 -> x12, local copies, waits for them, and re-layouts: 5.22 us -> 4.93 us
  transfers between devices with their start and end apart: 9 -> 9, of which waited for: 3 -> 2; matrix products, arithmetic and copies ran while one was open for 2% -> 3% of each run, Pallas kernels for 17% -> 14%
where the time goes in v1:
time: 61.6 us; the launch traced here: 61.9 us
  waiting for transfers between devices  25.9 us (42%)
  starting transfers between devices  16.8 us (27%)
  Pallas kernels  11 us (18%)
  local copies, waits for them, and re-layouts  5.45 us (9%)
  between operations  1.5 us (2%)
  other arithmetic  1.15 us (2%)
    ppermute x1, waiting for transfers between devices, relay_first(): return [first, lax.ppermute(third, 'ctx', [(3, 2), (2, 0)])]  15.1 us
    ppermute x1, waiting for transfers between devices, relay_first(): first = lax.ppermute(first, 'ctx', [(3, 2), (2, 1), (1, 0)])  10.8 us
    ppermute x2, starting transfers between devices, spread(): lax.ppermute(part, 'ctx', [(0, 2), (2, 3)])  9.43 us
    unnamed x12, local copies, waits for them, and re-layouts  4.93 us
    pallas_call x2, Pallas kernels, local_terms(): pl.pallas_call(functools.partial(local_kernel, part, key_head), out_shape...  3.89 us
    pallas_call x1, Pallas kernels, own_scores(): pl.pallas_call(functools.partial(own_kernel, 4), out_shape=(square, squar...  2.18 us
    ppermute x1, starting transfers between devices, spread(): gamma = lax.ppermute(sent + 0 * alpha[1][:1, :1], 'ctx', [(0, 1), (1, 2)])  1.93 us
    ppermute x1, starting transfers between devices, relay_first(): first = lax.ppermute(first, 'ctx', [(3, 2), (2, 1), (1, 0)])  1.47 us
  transfers between devices with their start and end apart: 9, of which 2 were waited for; matrix products, arithmetic and copies ran while one was open for 3% of the time, Pallas kernels for 14%

profile of v1, /device:TPU:0, one launch (start us, length us, event | category | flops | bytes accessed | tf_op | source)
XLA Modules:
  0.0 61.9 jit_solution(15928313936513907417)
XLA Ops:
  0.6 5.9 %collective-permute-start.1 = (bf16[256,256]{1,0:T(8,128)(2,1)}, bf16[256,256]{1,0:T(8,128)(2,1)S(1)}, u32[]{:S(2)}, u32[]{:S(2)}) collective-permute-start(bf16[256,256]{1,0:T(8,128)(2,1)} %bitcast.14), channel_id=1, source_target_pairs={{0,8},{8,12},{1,9},{9,13},{2,10},{10,14},{3,11},{11,15},{16,24},{2... | collective-permute-start | bytes 393224 | tf_op jit(solution)/shard_map/ppermute | solution.py:531
  6.6 0.9 %copy-done.2 = bf16[1,256,256]{2,1,0:T(8,128)(2,1)S(1)} copy-done((bf16[1,256,256]{2,1,0:T(8,128)(2,1)S(1)}, bf16[1,256,256]{2,1,0:T(8,128)(2,1)}, u32[]{:S(2)}) %copy-start.2) | copy-done | bytes 131096
  7.5 0.9 %copy-done.3 = bf16[1,256,256]{2,1,0:T(8,128)(2,1)S(1)} copy-done((bf16[1,256,256]{2,1,0:T(8,128)(2,1)S(1)}, bf16[1,256,256]{2,1,0:T(8,128)(2,1)}, u32[]{:S(2)}) %copy-start.3) | copy-done | bytes 131096
  8.4 0.7 %copy-done.4 = s32[1,512]{1,0:T(1,128)S(1)} copy-done((s32[1,512]{1,0:T(1,128)S(1)}, s32[1,512]{1,0:T(1,128)}, u32[]{:S(2)}) %copy-start.4) | copy-done | bytes 2072
  9.1 1.3 %prepare.1 = (s32[8]{0:T(128)S(1)}, f32[256,128]{1,0:T(8,128)S(1)}, f32[256,128]{1,0:T(8,128)S(1)}, bf16[256,512]{1,0:T(8,128)(2,1)S(1)}, bf16[256,256]{1,0:T(8,128)(2,1)S(1)}) custom-call(s32[1,512]{1,0:T(1,128)S(1)} %copy-done.4, bf16[256,256]{1,0:T(8,128)(2,1)S(1)} %bitcast.13, bf16[256,256]{1,0:T(8,128)(2,1)S(1)} %bitcast.15), custom_call_target="tpu_custom_call" | custom-call | tf_op jit(solution)/shard_map/prepare/pallas_call | solution.py:103
  10.4 3.5 %collective-permute-start = (bf16[256,256]{1,0:T(8,128)(2,1)S(1)}, bf16[256,256]{1,0:T(8,128)(2,1)S(1)}, u32[]{:S(2)}, u32[]{:S(2)}) collective-permute-start(bf16[256,256]{1,0:T(8,128)(2,1)S(1)} %get-tuple-element.30), channel_id=1, source_target_pairs={{0,8},{8,12},{1,9},{9,13},{2,10},{10,14},{3,11},{11,15},{16,24},{2... | collective-permute-start | bytes 393224 | tf_op jit(solution)/shard_map/ppermute | solution.py:531
  13.9 0.7 %collective-permute-start.2 = (bf16[256,512]{1,0:T(8,128)(2,1)S(1)}, bf16[256,512]{1,0:T(8,128)(2,1)S(1)}, u32[]{:S(2)}, u32[]{:S(2)}) collective-permute-start(bf16[256,512]{1,0:T(8,128)(2,1)S(1)} %get-tuple-element.32.sent_ref), channel_id=1, source_target_pairs={{4,12},{5,13},{6,14},{7,15},{20,28},{21,29},{22,30},{23,31}} | collective-permute-start | bytes 786440 | tf_op jit(solution)/shard_map/ppermute | solution.py:532
  14.6 0.5 slice.4
  15.8 1.9 %collective-permute-start.3 = (bf16[256,512]{1,0:T(8,128)(2,1)S(1)}, bf16[256,512]{1,0:T(8,128)(2,1)S(1)}, u32[]{:S(2)}, u32[]{:S(2)}) collective-permute-start(bf16[256,512]{1,0:T(8,128)(2,1)S(1)} %broadcast_add_fusion), channel_id=1, source_target_pairs={{0,4},{4,8},{1,5},{5,9},{2,6},{6,10},{3,7},{7,11},{16,20},{20,24},... | collective-permute-start | bytes 786440 | tf_op jit(solution)/shard_map/ppermute | solution.py:533
  17.7 0.7 %collective-permute-start.5 = (bf16[256,256]{1,0:T(8,128)(2,1)S(1)}, bf16[256,256]{1,0:T(8,128)(2,1)S(1)}, u32[]{:S(2)}, u32[]{:S(2)}) collective-permute-start(bf16[256,256]{1,0:T(8,128)(2,1)S(1)} %collective-permute-done.1.refs_1_), channel_id=1, source_target_pairs={{8,12},{9,13},{10,14},{11,15},{24,28},{25,29},{26,30},{27,31}} | collective-permute-start | bytes 393224 | tf_op jit(solution)/shard_map/ppermute | solution.py:534
  18.4 0.0 collective-permute-done.refs_0_
  18.4 0.7 %collective-permute-start.4 = (bf16[256,256]{1,0:T(8,128)(2,1)S(1)}, bf16[256,256]{1,0:T(8,128)(2,1)S(1)}, u32[]{:S(2)}, u32[]{:S(2)}) collective-permute-start(bf16[256,256]{1,0:T(8,128)(2,1)S(1)} %collective-permute-done.refs_0_), channel_id=1, source_target_pairs={{8,12},{9,13},{10,14},{11,15},{24,28},{25,29},{26,30},{27,31}} | collective-permute-start | bytes 393224 | tf_op jit(solution)/shard_map/ppermute | solution.py:534
  19.1 0.0 copy-start
  19.1 1.2 %copy-done = bf16[1,256,2048]{2,1,0:T(8,128)(2,1)S(1)} copy-done((bf16[1,256,2048]{2,1,0:T(8,128)(2,1)S(1)}, bf16[1,256,2048]{2,1,0:T(8,128)(2,1)}, u32[]{:S(2)}) %copy-start) | copy-done | bytes 1048600
  20.3 1.2 %copy-done.5 = bf16[1,256,2048]{2,1,0:T(8,128)(2,1)S(1)} copy-done((bf16[1,256,2048]{2,1,0:T(8,128)(2,1)S(1)}, bf16[1,256,2048]{2,1,0:T(8,128)(2,1)}, u32[]{:S(2)}) %copy-start.5) | copy-done | bytes 1048600
  21.5 1.2 %rotate_queries.1 = (bf16[256,2048]{1,0:T(8,128)(2,1)S(1)}, bf16[2048,256]{1,0:T(8,128)(2,1)S(1)}, bf16[2048,256]{1,0:T(8,128)(2,1)S(1)}) custom-call(f32[256,128]{1,0:T(8,128)S(1)} %get-tuple-element.28.cos_ref, f32[256,128]{1,0:T(8,128)S(1)} %get-tuple-element.29.sin_ref, bf16[256,2048]{1,0:T(8,128)(2,1)S(1)} %bitcast.16, bf16[256,2048]{1,0:T(8,128)(2,1)S(1)} %bitcast.9, ...), custom_call_target="tpu_custom_call" | custom-call | flops 3000000000 | bytes 4194304 | tf_op jit(solution)/shard_map/rotate_queries/pallas_call | solution.py:133
  22.7 0.0 copy-start.1
  22.7 2.2 %own_scores.1 = (f32[16,256,256]{2,1,0:T(8,128)S(1)}, f32[16,256,256]{2,1,0:T(8,128)S(1)}, f32[16,8,256]{2,1,0:T(8,128)S(1)}) custom-call(bf16[256,512]{1,0:T(8,128)(2,1)S(1)} %get-tuple-element.32.sent_ref, bf16[2048,256]{1,0:T(8,128)(2,1)S(1)} %get-tuple-element.33.turned_t_ref, bf16[2048,256]{1,0:T(8,128)(2,1)S(1)} %get-tuple-element.34.grad_t_ref), custom_call_target="tpu_custom_call" | custom-call | flops 5000000000 | bytes 10485760 | tf_op jit(solution)/shard_map/own_scores/pallas_call | solution.py:221
  24.9 0.0 collective-permute-done.4.refs_4_
  24.9 0.0 collective-permute-done.2.refs_2_
  25.0 1.0 %scores.1 = (bf16[256,512]{1,0:T(8,128)(2,1)S(1)}, bf16[256,512]{1,0:T(8,128)(2,1)S(1)}, f32[256,512]{1,0:T(8,128)S(1)}, bf16[576,4096]{1,0:T(8,128)(2,1)S(1)}, ...) custom-call(s32[8]{0:T(128)S(1)} %get-tuple-element.27.meta_ref, ...), custom_call_target="tpu_custom_call" | custom-call | flops 8000000000 | bytes 12582912 | tf_op jit(solution)/shard_map/scores/pallas_call | solution.py:381
  26.0 1.5 %collective-permute-start.6 = (bf16[256,512]{1,0:T(8,128)(2,1)S(1)}, bf16[256,512]{1,0:T(8,128)(2,1)S(1)}, u32[]{:S(2)}, u32[]{:S(2)}) collective-permute-start(bf16[256,512]{1,0:T(8,128)(2,1)S(1)} %get-tuple-element.44), channel_id=1, source_target_pairs={{12,8},{8,4},{4,0},{13,9},{9,5},{5,1},{14,10},{10,6},{6,2},{15,11}... | collective-permute-start | bytes 786440 | tf_op jit(solution)/shard_map/ppermute | solution.py:544
  27.5 1.9 %local_terms.2 = (bf16[256,1024]{1,0:T(8,128)(2,1)S(1)}, f32[256,256]{1,0:T(8,128)S(1)}, bf16[256,512]{1,0:T(8,128)(2,1)S(1)}) custom-call(s32[8]{0:T(128)S(1)} %get-tuple-element.27.meta_ref, f32[256,128]{1,0:T(8,128)S(1)} %get-tuple-element.28.cos_ref, f32[256,128]{1,0:T(8,128)S(1)} %get-tuple-element.29.sin_ref, ...), custom_call_target="tpu_custom_call" | custom-call | flops 4000000000 | bytes 10485760 | tf_op jit(solution)/shard_map/local_terms/pallas_call | solution.py:471
  29.4 0.7 %collective-permute-start.8 = (bf16[256,512]{1,0:T(8,128)(2,1)S(1)}, bf16[256,512]{1,0:T(8,128)(2,1)S(1)}, u32[]{:S(2)}, u32[]{:S(2)}) collective-permute-start(bf16[256,512]{1,0:T(8,128)(2,1)S(1)} %get-tuple-element.46), channel_id=1, source_target_pairs={{12,4},{13,5},{14,6},{15,7},{28,20},{29,21},{30,22},{31,23}} | collective-permute-start | bytes 786440 | tf_op jit(solution)/shard_map/ppermute | solution.py:609
  30.1 10.8 %collective-permute-done.6.refs_0_ = bf16[256,512]{1,0:T(8,128)(2,1)S(1)} collective-permute-done((bf16[256,512]{1,0:T(8,128)(2,1)S(1)}, bf16[256,512]{1,0:T(8,128)(2,1)S(1)}, u32[]{:S(2)}, u32[]{:S(2)}) %collective-permute-start.6) | collective-permute-done | bytes 262176 | tf_op jit(solution)/shard_map/ppermute | solution.py:544
  40.9 0.1 add_convert_fusion
  41.0 1.3 %collective-permute-start.7 = (bf16[256,512]{1,0:T(8,128)(2,1)S(1)}, bf16[256,512]{1,0:T(8,128)(2,1)S(1)}, u32[]{:S(2)}, u32[]{:S(2)}) collective-permute-start(bf16[256,512]{1,0:T(8,128)(2,1)S(1)} %add_convert_fusion), channel_id=1, source_target_pairs={{12,8},{8,0},{13,9},{9,1},{14,10},{10,2},{15,11},{11,3},{28,24},{2... | collective-permute-start | bytes 786440 | tf_op jit(solution)/shard_map/ppermute | solution.py:546
  42.3 1.9 %local_terms.3 = (bf16[256,1024]{1,0:T(8,128)(2,1)S(1)}, f32[256,256]{1,0:T(8,128)S(1)}) custom-call(s32[8]{0:T(128)S(1)} %get-tuple-element.27.meta_ref, f32[256,128]{1,0:T(8,128)S(1)} %get-tuple-element.28.cos_ref, f32[256,128]{1,0:T(8,128)S(1)} %get-tuple-element.29.sin_ref, bf16[256,2048]{1,0:T(8,128)(2,1)S(1)} %get-tuple-element.31.turned_ref, ...), custom_call_target="tpu_custom_call" | custom-call | flops 4000000000 | bytes 10485760 | tf_op jit(solution)/shard_map/local_terms/pallas_call | solution.py:471
  44.3 1.1 %maximum_bitcast_fusion = bf16[1,256,2048]{2,1,0:T(8,128)(2,1)} fusion(bf16[256,1024]{1,0:T(8,128)(2,1)S(1)} %get-tuple-element.43, bf16[256,1024]{1,0:T(8,128)(2,1)S(1)} %get-tuple-element.42), kind=kLoop, calls=%fused_computation | loop fusion | flops 2097152 | bytes 2097152 | tf_op jit(solution)/shard_map/broadcast_in_dim | solution.py:613
  45.3 0.0 collective-permute-done.8.refs_2_
  45.3 15.1 %collective-permute-done.7.refs_1_ = bf16[256,512]{1,0:T(8,128)(2,1)S(1)} collective-permute-done((bf16[256,512]{1,0:T(8,128)(2,1)S(1)}, bf16[256,512]{1,0:T(8,128)(2,1)S(1)}, u32[]{:S(2)}, u32[]{:S(2)}) %collective-permute-start.7) | collective-permute-done | bytes 262176 | tf_op jit(solution)/shard_map/ppermute | solution.py:546
  60.4 1.4 %finish.1 = (bf16[256,256]{1,0:T(8,128)(2,1)}, bf16[256,256]{1,0:T(8,128)(2,1)}) custom-call(s32[8]{0:T(128)S(1)} %get-tuple-element.27.meta_ref, f32[256,128]{1,0:T(8,128)S(1)} %get-tuple-element.28.cos_ref, f32[256,128]{1,0:T(8,128)S(1)} %get-tuple-element.29.sin_ref, bf16[256,512]{1,0:T(8,128)(2,1)S(1)} %collective-permute-done.6.refs_0_, ...), custom_call_target="tpu_custom_call" | custom-call | tf_op jit(solution)/shard_map/finish/pallas_call | solution.py:515
  (9 shorter events, 0.0 us)
Async XLA Ops:
  0.6 13.9 %collective-permute-start.1 = (bf16[256,256]{1,0:T(8,128)(2,1)}, bf16[256,256]{1,0:T(8,128)(2,1)S(1)}, u32[]{:S(2)}, u32[]{:S(2)}) collective-permute-start(bf16[256,256]{1,0:T(8,128)(2,1)} %bitcast.14), channel_id=1, source_target_pairs={{0,8},{8,12},{1,9},{9,13},{2,10},{10,14},{3,11},{11,15},{16,24},{2... | collective-permute-start | bytes 393224 | tf_op jit(solution)/shard_map/ppermute | solution.py:531
  6.6 0.9 %copy-start.2 = (bf16[1,256,256]{2,1,0:T(8,128)(2,1)S(1)}, bf16[1,256,256]{2,1,0:T(8,128)(2,1)}, u32[]{:S(2)}) copy-start(bf16[1,256,256]{2,1,0:T(8,128)(2,1)} %param.7) | copy-start | bytes 393220
  7.5 0.9 %copy-start.3 = (bf16[1,256,256]{2,1,0:T(8,128)(2,1)S(1)}, bf16[1,256,256]{2,1,0:T(8,128)(2,1)}, u32[]{:S(2)}) copy-start(bf16[1,256,256]{2,1,0:T(8,128)(2,1)} %param.8) | copy-start | bytes 393220
  8.4 0.7 %copy-start.4 = (s32[1,512]{1,0:T(1,128)S(1)}, s32[1,512]{1,0:T(1,128)}, u32[]{:S(2)}) copy-start(s32[1,512]{1,0:T(1,128)} %pos_ref.1) | copy-start | bytes 6148
  10.4 8.0 %collective-permute-start = (bf16[256,256]{1,0:T(8,128)(2,1)S(1)}, bf16[256,256]{1,0:T(8,128)(2,1)S(1)}, u32[]{:S(2)}, u32[]{:S(2)}) collective-permute-start(bf16[256,256]{1,0:T(8,128)(2,1)S(1)} %get-tuple-element.30), channel_id=1, source_target_pairs={{0,8},{8,12},{1,9},{9,13},{2,10},{10,14},{3,11},{11,15},{16,24},{2... | collective-permute-start | bytes 393224 | tf_op jit(solution)/shard_map/ppermute | solution.py:531
  13.9 11.1 %collective-permute-start.2 = (bf16[256,512]{1,0:T(8,128)(2,1)S(1)}, bf16[256,512]{1,0:T(8,128)(2,1)S(1)}, u32[]{:S(2)}, u32[]{:S(2)}) collective-permute-start(bf16[256,512]{1,0:T(8,128)(2,1)S(1)} %get-tuple-element.32.sent_ref), channel_id=1, source_target_pairs={{4,12},{5,13},{6,14},{7,15},{20,28},{21,29},{22,30},{23,31}} | collective-permute-start | bytes 786440 | tf_op jit(solution)/shard_map/ppermute | solution.py:532
  15.8 9.2 %collective-permute-start.3 = (bf16[256,512]{1,0:T(8,128)(2,1)S(1)}, bf16[256,512]{1,0:T(8,128)(2,1)S(1)}, u32[]{:S(2)}, u32[]{:S(2)}) collective-permute-start(bf16[256,512]{1,0:T(8,128)(2,1)S(1)} %broadcast_add_fusion), channel_id=1, source_target_pairs={{0,4},{4,8},{1,5},{5,9},{2,6},{6,10},{3,7},{7,11},{16,20},{20,24},... | collective-permute-start | bytes 786440 | tf_op jit(solution)/shard_map/ppermute | solution.py:533
  17.7 7.2 %collective-permute-start.5 = (bf16[256,256]{1,0:T(8,128)(2,1)S(1)}, bf16[256,256]{1,0:T(8,128)(2,1)S(1)}, u32[]{:S(2)}, u32[]{:S(2)}) collective-permute-start(bf16[256,256]{1,0:T(8,128)(2,1)S(1)} %collective-permute-done.1.refs_1_), channel_id=1, source_target_pairs={{8,12},{9,13},{10,14},{11,15},{24,28},{25,29},{26,30},{27,31}} | collective-permute-start | bytes 393224 | tf_op jit(solution)/shard_map/ppermute | solution.py:534
  18.4 6.5 %collective-permute-start.4 = (bf16[256,256]{1,0:T(8,128)(2,1)S(1)}, bf16[256,256]{1,0:T(8,128)(2,1)S(1)}, u32[]{:S(2)}, u32[]{:S(2)}) collective-permute-start(bf16[256,256]{1,0:T(8,128)(2,1)S(1)} %collective-permute-done.refs_0_), channel_id=1, source_target_pairs={{8,12},{9,13},{10,14},{11,15},{24,28},{25,29},{26,30},{27,31}} | collective-permute-start | bytes 393224 | tf_op jit(solution)/shard_map/ppermute | solution.py:534
  19.1 1.2 %copy-start = (bf16[1,256,2048]{2,1,0:T(8,128)(2,1)S(1)}, bf16[1,256,2048]{2,1,0:T(8,128)(2,1)}, u32[]{:S(2)}) copy-start(bf16[1,256,2048]{2,1,0:T(8,128)(2,1)} %param.9) | copy-start | bytes 3145732
  20.3 1.2 %copy-start.5 = (bf16[1,256,2048]{2,1,0:T(8,128)(2,1)S(1)}, bf16[1,256,2048]{2,1,0:T(8,128)(2,1)}, u32[]{:S(2)}) copy-start(bf16[1,256,2048]{2,1,0:T(8,128)(2,1)} %param.6) | copy-start | bytes 3145732
  22.7 2.2 %copy-start.1 = (bf16[1,256,2048]{2,1,0:T(8,128)(2,1)S(1)}, bf16[1,256,2048]{2,1,0:T(8,128)(2,1)}, u32[]{:S(2)}) copy-start(bf16[1,256,2048]{2,1,0:T(8,128)(2,1)} %param.9) | copy-start | bytes 3145732
  26.0 14.9 %collective-permute-start.6 = (bf16[256,512]{1,0:T(8,128)(2,1)S(1)}, bf16[256,512]{1,0:T(8,128)(2,1)S(1)}, u32[]{:S(2)}, u32[]{:S(2)}) collective-permute-start(bf16[256,512]{1,0:T(8,128)(2,1)S(1)} %get-tuple-element.44), channel_id=1, source_target_pairs={{12,8},{8,4},{4,0},{13,9},{9,5},{5,1},{14,10},{10,6},{6,2},{15,11}... | collective-permute-start | bytes 786440 | tf_op jit(solution)/shard_map/ppermute | solution.py:544
  29.4 15.9 %collective-permute-start.8 = (bf16[256,512]{1,0:T(8,128)(2,1)S(1)}, bf16[256,512]{1,0:T(8,128)(2,1)S(1)}, u32[]{:S(2)}, u32[]{:S(2)}) collective-permute-start(bf16[256,512]{1,0:T(8,128)(2,1)S(1)} %get-tuple-element.46), channel_id=1, source_target_pairs={{12,4},{13,5},{14,6},{15,7},{28,20},{29,21},{30,22},{31,23}} | collective-permute-start | bytes 786440 | tf_op jit(solution)/shard_map/ppermute | solution.py:609
  41.0 19.4 %collective-permute-start.7 = (bf16[256,512]{1,0:T(8,128)(2,1)S(1)}, bf16[256,512]{1,0:T(8,128)(2,1)S(1)}, u32[]{:S(2)}, u32[]{:S(2)}) collective-permute-start(bf16[256,512]{1,0:T(8,128)(2,1)S(1)} %add_convert_fusion), channel_id=1, source_target_pairs={{12,8},{8,0},{13,9},{9,1},{14,10},{10,2},{15,11},{11,3},{28,24},{2... | collective-permute-start | bytes 786440 | tf_op jit(solution)/shard_map/ppermute | solution.py:546
